TPU v7x, 32 devices: a whole 2x2x4 slice. The times are simulated.
32 devices in a mesh: pipe: 2 (over core), seq: 4 (over z), tensor: 4 (over y, x).
Axes of the slice: x: 2, y: 2, z: 4, core: 2. Of those that a mesh axis runs over, the one named last changes fastest.
Arguments:
- frames: bfloat16 [2, 2560, 768], P(None, ('seq', 'tensor')), may hold values from -6 to 6
- clip_ids: int32 [2, 2560], P(None, 'seq'), may hold values from 0 to 2, as said below
- cotangent: bfloat16 [2, 2560, 768], P(None, ('seq', 'tensor')), may hold values from -6 to 6
- norm_gains: float32 [2, 2, 768], P('pipe'), may hold values from 0.25 to 1.75
- norm_shifts: float32 [2, 4, 768], P('pipe'), may hold values from -1.5 to 1.5
- query_projection_weight: bfloat16 [2, 768, 768], P('pipe', None, 'tensor'), may hold values from -0.4375 to 0.4375
- w_keyval: bfloat16 [2, 2, 768, 768], P('pipe', None, None, 'tensor'), may hold values from -0.21875 to 0.21875
- proj_bias: float32 [2, 2, 768], P('pipe', None, 'tensor'), may hold values from -0.3 to 0.3
- w_output: bfloat16 [2, 768, 768], P('pipe', 'tensor'), may hold values from -3 to 3
- w_expand: bfloat16 [2, 768, 3072], P('pipe', None, 'tensor'), may hold values from -0.21875 to 0.21875
- expand_bias: float32 [2, 3072], P('pipe', 'tensor'), may hold values from -2.5 to 2.5
- w_reduce: bfloat16 [2, 3072, 768], P('pipe', 'tensor'), may hold values from -0.109375 to 0.109375
Outputs:
- states: bfloat16 [2, 2, 2560, 768], P('pipe', None, ('seq', 'tensor'))
- input_grads: bfloat16 [2, 2, 2560, 768], P('pipe', None, ('seq', 'tensor'))
- grad_gains: float32 [2, 2, 768], P('pipe')
- grad_shifts: float32 [2, 4, 768], P('pipe')
- grad_query: float32 [2, 768, 768], P('pipe', None, 'tensor')
- grad_keyval: float32 [2, 2, 768, 768], P('pipe', None, None, 'tensor')
- grad_proj_bias: float32 [2, 2, 768], P('pipe', None, 'tensor')
- grad_output: float32 [2, 768, 768], P('pipe', 'tensor')
- grad_expand: float32 [2, 768, 3072], P('pipe', None, 'tensor')
- grad_expand_bias: float32 [2, 3072], P('pipe', 'tensor')
- grad_reduce: float32 [2, 3072, 768], P('pipe', 'tensor')
Inputs may be any that keep to these rules, and one draw needn't show every extreme that they name: `clip_ids`: in each micro-batch the ids start at 0, never fall, and rise by one at the first frame of each clip; every clip has exactly 1500 frames except the first and the last of a micro-batch, which may have fewer; each micro-batch holds at least one whole clip; the largest id of some micro-batch is (2).
All inputs are finite; a program needn't handle non-finite values.
Results may differ from a plain program's by a relative error of at most 0.035.
Values may be sent and summed in bfloat16 or wider, within the bound.
A program may use at most 128 MiB of HBM per device.

v0:
```python
import jax
import jax.numpy as jnp
from jax import lax
from jax.sharding import PartitionSpec as P

HEAD_DIM = 64
REACH = 3


EPS = 1e-05
NEG = -1e30


def shifted(block, axis, distance):
    devices = range(lax.axis_size(axis))
    route = [(i - distance, i) for i in devices if i - distance in devices]
    return lax.ppermute(block, axis, route)


def norm_rows(values_in, gain, shift):
    center = values_in - jnp.mean(values_in, axis=-1, keepdims=True)
    spread = jnp.mean(center * center, axis=-1, keepdims=True)
    return center * lax.rsqrt(spread + EPS) * gain + shift


def gelu_exact(values_in):
    return jax.nn.gelu(values_in, approximate=False)


def matmul(left, right):
    return jnp.dot(left, right, preferred_element_type=jnp.float32)


def inner_rows(left, right):
    return lax.dot_general(
        left, right, (((0,), (0,)), ((), ())), preferred_element_type=jnp.float32
    )


def times_trans(left, right):
    return lax.dot_general(
        left, right, (((1,), (1,)), ((), ())), preferred_element_type=jnp.float32
    )


def split_heads(matrix):
    return matrix.reshape(matrix.shape[0], -1, HEAD_DIM)


def window_heads(matrix_win):
    return matrix_win.reshape(matrix_win.shape[0], matrix_win.shape[1], -1, HEAD_DIM)


def offsets_list():
    return list(range(REACH, -REACH - 1, -1))


def spread_rows(piece):
    return lax.all_gather(piece, "tensor", axis=0, tiled=True)


def fold_rows(partial_sum):
    return lax.psum_scatter(
        partial_sum.astype(jnp.bfloat16), "tensor", scatter_dimension=0, tiled=True
    ).astype(jnp.float32)


def neighbour_kv(pieces, offset):
    return shifted((pieces[0], pieces[1], pieces[2]), "seq", offset)


def return_terms(pieces, offset):
    return (
        shifted(pieces[0].astype(jnp.bfloat16), "seq", offset).astype(jnp.float32),
        shifted(pieces[1].astype(jnp.bfloat16), "seq", offset).astype(jnp.float32),
    )


def gather_window(keys_here, values_here, mark_here):
    keys_list = []
    values_list = []
    marks_list = []
    for offset in offsets_list():
        if offset == 0:
            got = (keys_here, values_here, mark_here)
        else:
            got = neighbour_kv((keys_here, values_here, mark_here), offset)
        keys_list.append(got[0])
        values_list.append(got[1])
        marks_list.append(got[2])
    return (jnp.stack(keys_list), jnp.stack(values_list), jnp.stack(marks_list))


def masked_scores(query_heads, key_heads, clip_query, clip_keys):
    factor = HEAD_DIM ** (-0.5)
    scores = (
        jnp.einsum("qhd,khd->hqk", query_heads, key_heads, preferred_element_type=jnp.float32)
        * factor
    )
    same_clip = (clip_query[:, None] == clip_keys[None, :])[None]
    return (scores, same_clip)


def block_grads(
    query_heads, grad_heads, log_total, delta, clip_query, key_heads, value_heads, clip_keys
):
    scores, same_clip = masked_scores(query_heads, key_heads, clip_query, clip_keys)
    probs = jnp.where(same_clip, jnp.exp(scores - log_total[..., None]), 0.0)
    grad_probs = jnp.einsum(
        "qhd,khd->hqk", grad_heads, value_heads, preferred_element_type=jnp.float32
    )
    grad_scores = (probs * (grad_probs - delta[..., None])).astype(jnp.bfloat16)
    return (probs.astype(jnp.bfloat16), grad_scores)


def forward_attention(query, keys_win, values_win, mark_here, marks_win):
    row_count = query.shape[0]
    query_heads = split_heads(query)
    head_count = query_heads.shape[1]
    key_blocks = window_heads(keys_win)
    value_blocks = window_heads(values_win)

    def first_pass(carry, items):
        row_max, row_sum = carry
        key_heads, clip_keys = items
        scores, same_clip = masked_scores(query_heads, key_heads, mark_here, clip_keys)
        scores = jnp.where(same_clip, scores, NEG)
        new_max = jnp.maximum(row_max, jnp.max(scores, axis=-1))
        weights = jnp.where(same_clip, jnp.exp(scores - new_max[..., None]), 0.0)
        row_sum = row_sum * jnp.exp(row_max - new_max) + jnp.sum(weights, axis=-1)
        return ((new_max, row_sum), None)

    start_max = jnp.full((head_count, row_count), NEG, jnp.float32)
    start_sum = jnp.zeros((head_count, row_count), jnp.float32)
    (row_max, row_sum), _ = lax.scan(first_pass, (start_max, start_sum), (key_blocks, marks_win))
    log_total = row_max + jnp.log(row_sum)

    def second_pass(carry, items):
        key_heads, value_heads, clip_keys = items
        scores, same_clip = masked_scores(query_heads, key_heads, mark_here, clip_keys)
        probs = jnp.where(same_clip, jnp.exp(scores - log_total[..., None]), 0.0).astype(
            jnp.bfloat16
        )
        return (
            carry
            + jnp.einsum("hqk,khd->qhd", probs, value_heads, preferred_element_type=jnp.float32),
            None,
        )

    start_mix = jnp.zeros((row_count, head_count, HEAD_DIM), jnp.float32)
    mixed, _ = lax.scan(second_pass, start_mix, (key_blocks, value_blocks, marks_win))
    return (mixed.reshape(row_count, -1), log_total)


def backward_attention(saved_activation, grad_mixed):
    factor = HEAD_DIM ** (-0.5)
    query_heads = split_heads(saved_activation["query"])
    grad_heads = split_heads(grad_mixed)
    mixed_heads = split_heads(saved_activation["mixed"])
    row_count = query_heads.shape[0]
    head_count = query_heads.shape[1]
    delta_rows = jnp.sum(grad_heads.astype(jnp.float32) * mixed_heads.astype(jnp.float32), axis=-1)
    delta = delta_rows.T
    log_total = saved_activation["log_total"]
    mark_here = saved_activation["mark_here"]
    key_blocks = window_heads(saved_activation["keys_win"])
    value_blocks = window_heads(saved_activation["values_win"])
    marks_win = saved_activation["marks_win"]
    start_query = jnp.zeros((row_count, head_count, HEAD_DIM), jnp.float32)

    def back_block(grad_query, items):
        key_heads, value_heads, clip_keys = items
        probs, grad_scores = block_grads(
            query_heads, grad_heads, log_total, delta, mark_here, key_heads, value_heads, clip_keys
        )
        grad_query = grad_query + factor * jnp.einsum(
            "hqk,khd->qhd", grad_scores, key_heads, preferred_element_type=jnp.float32
        )
        key_term = factor * jnp.einsum(
            "hqk,qhd->khd", grad_scores, query_heads, preferred_element_type=jnp.float32
        )
        value_term = jnp.einsum(
            "hqk,qhd->khd", probs, grad_heads, preferred_element_type=jnp.float32
        )
        return (grad_query, (key_term, value_term))

    grad_query, (key_terms, value_terms) = lax.scan(
        back_block, start_query, (key_blocks, value_blocks, marks_win)
    )
    grad_keys = jnp.zeros((row_count, head_count * HEAD_DIM), jnp.float32)
    grad_values = jnp.zeros((row_count, head_count * HEAD_DIM), jnp.float32)
    for place, offset in enumerate(offsets_list()):
        pair = (key_terms[place].reshape(row_count, -1), value_terms[place].reshape(row_count, -1))
        if offset != 0:
            pair = return_terms(pair, -offset)
        grad_keys = grad_keys + pair[0]
        grad_values = grad_values + pair[1]
    return (grad_query.reshape(row_count, -1), grad_keys, grad_values)


def layer_forward(layer_in, clip_here, weights):
    gains, shifts, query_weight, keyval_w, bias_pair, output_w, expand_w, expand_b, reduce_w = (
        weights
    )
    resid_in = layer_in.astype(jnp.float32)
    normed = spread_rows(norm_rows(resid_in, gains[0], shifts[0]).astype(jnp.bfloat16))
    query = (matmul(normed, query_weight) + bias_pair[0]).astype(jnp.bfloat16)
    keys_here = matmul(normed, keyval_w[0]).astype(jnp.bfloat16)
    values_here = (matmul(normed, keyval_w[1]) + bias_pair[1]).astype(jnp.bfloat16)
    mark_here = clip_here + 1
    keys_win, values_win, marks_win = gather_window(keys_here, values_here, mark_here)
    mixed, log_total = forward_attention(query, keys_win, values_win, mark_here, marks_win)
    mixed = mixed.astype(jnp.bfloat16)
    resid_mid = resid_in + fold_rows(matmul(mixed, output_w)) + shifts[2]
    normed_mid = spread_rows(norm_rows(resid_mid, gains[1], shifts[1]).astype(jnp.bfloat16))
    expanded = matmul(normed_mid, expand_w) + expand_b
    activated = gelu_exact(expanded).astype(jnp.bfloat16)
    layer_out = (resid_mid + fold_rows(matmul(activated, reduce_w)) + shifts[3]).astype(
        jnp.bfloat16
    )
    saved_activation = {
        "layer_in": layer_in,
        "normed": normed,
        "query": query,
        "keys_here": keys_here,
        "values_here": values_here,
        "keys_win": keys_win,
        "values_win": values_win,
        "mark_here": mark_here,
        "marks_win": marks_win,
        "mixed": mixed,
        "log_total": log_total,
        "resid_mid": resid_mid,
        "normed_mid": normed_mid,
        "expanded": expanded,
        "activated": activated,
    }
    return (layer_out, saved_activation)


def layer_backward(layer_grad, saved_activation, weights):
    gains, shifts, query_weight, keyval_w, bias_pair, output_w, expand_w, expand_b, reduce_w = (
        weights
    )
    grad_out = layer_grad.astype(jnp.float32)
    grad_all = spread_rows(layer_grad)
    grad_reduce = inner_rows(saved_activation["activated"], grad_all)
    grad_act = times_trans(grad_all, reduce_w)
    gelu_back = jax.vjp(gelu_exact, saved_activation["expanded"])[1]
    grad_expanded = gelu_back(grad_act)[0].astype(jnp.bfloat16)
    grad_expand_bias = jnp.sum(grad_expanded, axis=0, dtype=jnp.float32)
    grad_expand = inner_rows(saved_activation["normed_mid"], grad_expanded)
    grad_normed_mid = fold_rows(times_trans(grad_expanded, expand_w))
    mid_back = jax.vjp(norm_rows, saved_activation["resid_mid"], gains[1], shifts[1])[1]
    grad_mid_norm, grad_gain_mid, grad_shift_mid = mid_back(grad_normed_mid)
    grad_mid = grad_out + grad_mid_norm
    grad_branch = spread_rows(grad_mid.astype(jnp.bfloat16))
    grad_output = inner_rows(saved_activation["mixed"], grad_branch)
    grad_mixed = times_trans(grad_branch, output_w).astype(jnp.bfloat16)
    grad_query, grad_keys, grad_values = backward_attention(saved_activation, grad_mixed)
    grad_query = grad_query.astype(jnp.bfloat16)
    grad_keys = grad_keys.astype(jnp.bfloat16)
    grad_values = grad_values.astype(jnp.bfloat16)
    grad_bias = jnp.stack(
        [
            jnp.sum(grad_query, axis=0, dtype=jnp.float32),
            jnp.sum(grad_values, axis=0, dtype=jnp.float32),
        ]
    )
    normed = saved_activation["normed"]
    grad_query_w = inner_rows(normed, grad_query)
    grad_keyval = jnp.stack([inner_rows(normed, grad_keys), inner_rows(normed, grad_values)])
    grad_normed = fold_rows(
        times_trans(grad_query, query_weight)
        + times_trans(grad_keys, keyval_w[0])
        + times_trans(grad_values, keyval_w[1])
    )
    in_back = jax.vjp(
        norm_rows, saved_activation["layer_in"].astype(jnp.float32), gains[0], shifts[0]
    )[1]
    grad_in_norm, grad_gain_in, grad_shift_in = in_back(grad_normed)
    input_grad = (grad_mid + grad_in_norm).astype(jnp.bfloat16)
    terms = {
        "gains": jnp.stack([grad_gain_in, grad_gain_mid]),
        "shifts": jnp.stack(
            [grad_shift_in, grad_shift_mid, jnp.sum(grad_mid, axis=0), jnp.sum(grad_out, axis=0)]
        ),
        "query": grad_query_w,
        "keyval": grad_keyval,
        "proj": grad_bias,
        "output": grad_output,
        "expand": grad_expand,
        "expand_bias": grad_expand_bias,
        "reduce": grad_reduce,
    }
    return (input_grad, terms)


def shards(
    frames,
    clip_ids,
    cotangent,
    norm_gains,
    norm_shifts,
    query_projection_weight,
    w_keyval,
    proj_bias,
    w_output,
    w_expand,
    expand_bias,
    w_reduce,
):
    weights = tuple(
        (
            member[0]
            for member in (
                norm_gains,
                norm_shifts,
                query_projection_weight,
                w_keyval,
                proj_bias,
                w_output,
                w_expand,
                expand_bias,
                w_reduce,
            )
        )
    )
    batch_groups = frames.shape[0]
    first_section = lax.axis_index("pipe") == 0
    received = jnp.zeros_like(frames[0])
    outputs_list = []
    saved_activations = []
    for current_step in range(batch_groups + 1):
        own_batch = min(current_step, batch_groups - 1)
        late_batch = max(current_step - 1, 0)
        layer_in = jnp.where(first_section, frames[own_batch], received)
        clip_here = jnp.where(first_section, clip_ids[own_batch], clip_ids[late_batch])
        layer_out, saved_activation = layer_forward(layer_in, clip_here, weights)
        outputs_list.append(layer_out)
        saved_activations.append(saved_activation)
        if current_step < batch_groups:
            received = shifted(layer_out, "pipe", 1)
    states = jnp.stack(
        [
            jnp.where(first_section, outputs_list[number], outputs_list[number + 1])
            for number in range(batch_groups)
        ]
    )[None]
    returned = jnp.zeros_like(cotangent[0])
    totals = None
    grads_list = []
    for current_step in range(batch_groups + 1):
        layer_grad = jnp.where(
            first_section, returned, cotangent[min(current_step, batch_groups - 1)]
        )
        prior_section = saved_activations[max(current_step - 1, 0)]
        next_section = saved_activations[min(current_step + 1, batch_groups)]
        saved_activation = jax.tree.map(
            lambda left, right: jnp.where(first_section, left, right), prior_section, next_section
        )
        valid = jnp.where(first_section, current_step >= 1, current_step < batch_groups)
        input_grad, terms = layer_backward(layer_grad, saved_activation, weights)
        terms = jax.tree.map(lambda item: jnp.where(valid, item, 0.0), terms)
        totals = terms if totals is None else jax.tree.map(jnp.add, totals, terms)
        grads_list.append(input_grad)
        if current_step < batch_groups:
            returned = shifted(input_grad, "pipe", -1)
    input_grads = jnp.stack(
        [
            jnp.where(first_section, grads_list[number + 1], grads_list[number])
            for number in range(batch_groups)
        ]
    )[None]
    summed = (
        lax.psum(totals["query"].astype(jnp.bfloat16), "seq").astype(jnp.float32),
        lax.psum(totals["keyval"].astype(jnp.bfloat16), "seq").astype(jnp.float32),
        lax.psum(totals["proj"].astype(jnp.bfloat16), "seq").astype(jnp.float32),
        lax.psum(totals["output"].astype(jnp.bfloat16), "seq").astype(jnp.float32),
        lax.psum(totals["expand"].astype(jnp.bfloat16), "seq").astype(jnp.float32),
        lax.psum(totals["expand_bias"].astype(jnp.bfloat16), "seq").astype(jnp.float32),
        lax.psum(totals["reduce"].astype(jnp.bfloat16), "seq").astype(jnp.float32),
    )
    vectors = lax.psum((totals["gains"], totals["shifts"]), ("seq", "tensor"))
    return (
        states,
        input_grads,
        vectors[0][None],
        vectors[1][None],
        summed[0][None],
        summed[1][None],
        summed[2][None],
        summed[3][None],
        summed[4][None],
        summed[5][None],
        summed[6][None],
    )


def solution(mesh):
    return jax.shard_map(
        shards,
        mesh=mesh,
        in_specs=(
            P(None, ("seq", "tensor"), None),
            P(None, "seq"),
            P(None, ("seq", "tensor"), None),
            P("pipe", None, None),
            P("pipe", None, None),
            P("pipe", None, "tensor"),
            P("pipe", None, None, "tensor"),
            P("pipe", None, "tensor"),
            P("pipe", "tensor", None),
            P("pipe", None, "tensor"),
            P("pipe", "tensor"),
            P("pipe", "tensor", None),
        ),
        out_specs=(
            P("pipe", None, ("seq", "tensor"), None),
            P("pipe", None, ("seq", "tensor"), None),
            P("pipe", None, None),
            P("pipe", None, None),
            P("pipe", None, "tensor"),
            P("pipe", None, None, "tensor"),
            P("pipe", None, "tensor"),
            P("pipe", "tensor", None),
            P("pipe", None, "tensor"),
            P("pipe", "tensor"),
            P("pipe", "tensor", None),
        ),
        check_vma=False,
    )
```

profile of v0, /device:TPU:0, one launch (start us, length us, event | category | flops | bytes accessed | tf_op | source)
XLA Modules:
  0.0 1702.6 jit_solution(10309989731337308341)
XLA Ops:
  83.2 62.9 %while.117 = (s32[]{:T(128)}, f32[3,640]{1,0:T(4,128)S(1)}, f32[3,640]{1,0:T(4,128)S(1)}, s32[640]{0:T(1024)S(1)}, s32[7,640]{1,0:T(8,128)}, /*index=5*/bf16[7,6...) while((s32[]{:T(128)}, f32[3,640]{1,0:T(4,128)S(1)}, ...), condition=%wide.region_5.6_spmd.clone, body=%wide.region_2.5_spmd.clone.sunk | while | flops 167536000 | bytes 11661420 | solution.py:135
  159.1 42.5 %while.118 = (s32[]{:T(128)}, f32[640,3,64]{0,2,1:T(8,128)}, bf16[7,640,3,64]{1,3,2,0:T(8,128)(2,1)}, s32[640]{0:T(1024)S(1)}, s32[7,640]{1,0:T(8,128)}, /*index...) while((s32[]{:T(128)}, f32[640,3,64]{0,2,1:T(8,128)}, ...), condition=%wide.region_7.8_spmd.clone, body=%wide.region_6.7_spmd.clone.sunk | while | flops 320143360 | bytes 3543671 | solution.py:151
  204.2 24.6 %reduce-scatter.13.cloned.1.call-done = bf16[160,768]{1,0:T(8,128)(2,1)} async-done(((bf16[640,768]{1,0:T(8,128)(2,1)}), bf16[160,768]{1,0:T(8,128)(2,1)}) %reduce-scatter.13.cloned.1.call-update) | async-done | bytes 245776 | tf_op jit(solution)/shard_map/reduce_scatter | solution.py:63
  254.2 27.4 %reduce-scatter.15.cloned.1.call-done = bf16[160,768]{1,0:T(8,128)(2,1)} async-done(((bf16[640,768]{1,0:T(8,128)(2,1)}), bf16[160,768]{1,0:T(8,128)(2,1)}) %reduce-scatter.15.cloned.1.call-update) | async-done | bytes 245776 | tf_op jit(solution)/shard_map/reduce_scatter | solution.py:63
  307.3 13.1 all_gather.38
  356.0 62.9 %while.119 = (s32[]{:T(128)}, f32[3,640]{1,0:T(4,128)S(1)}, f32[3,640]{1,0:T(4,128)S(1)}, s32[640]{0:T(1024)S(1)}, s32[7,640]{1,0:T(8,128)}, /*index=5*/bf16[7,6...) while((s32[]{:T(128)}, f32[3,640]{1,0:T(4,128)S(1)}, ...), condition=%wide.region_17.18_spmd.clone, body=%wide.region_14.17_spmd.clone.sunk | while | flops 167536000 | bytes 11661420 | solution.py:135
  432.2 49.4 %while.120 = (s32[]{:T(128)}, f32[640,3,64]{0,2,1:T(8,128)}, bf16[7,640,3,64]{1,3,2,0:T(8,128)(2,1)}, s32[640]{0:T(1024)S(1)}, s32[7,640]{1,0:T(8,128)}, /*index...) while((s32[]{:T(128)}, f32[640,3,64]{0,2,1:T(8,128)}, ...), condition=%wide.region_19.20_spmd.clone, body=%wide.region_18.19_spmd.clone.sunk | while | flops 320143360 | bytes 3950711 | solution.py:151
  484.2 24.7 %reduce-scatter.17.cloned.1.call-done = bf16[160,768]{1,0:T(8,128)(2,1)} async-done(((bf16[640,768]{1,0:T(8,128)(2,1)}), bf16[160,768]{1,0:T(8,128)(2,1)}) %reduce-scatter.17.cloned.1.call-update) | async-done | bytes 245776 | tf_op jit(solution)/shard_map/reduce_scatter | solution.py:63
  545.1 16.4 reduce-scatter.19.cloned.1.call-done
  638.9 57.8 %while.121 = (s32[]{:T(128)}, f32[3,640]{1,0:T(4,128)S(1)}, f32[3,640]{1,0:T(4,128)S(1)}, s32[640]{0:T(1024)S(1)}, s32[7,640]{1,0:T(8,128)S(1)}, /*index=5*/bf16...) while((s32[]{:T(128)}, f32[3,640]{1,0:T(4,128)S(1)}, ...), condition=%wide.region_29.30_spmd.clone, body=%wide.region_26.29_spmd.clone.sunk | while | flops 167536000 | bytes 11661420 | solution.py:135
  710.2 44.4 %while.122 = (s32[]{:T(128)}, f32[640,3,64]{0,2,1:T(8,128)}, bf16[7,640,3,64]{1,3,2,0:T(8,128)(2,1)}, s32[640]{0:T(1024)S(1)}, s32[7,640]{1,0:T(8,128)S(1)}, /*i...) while((s32[]{:T(128)}, f32[640,3,64]{0,2,1:T(8,128)}, ...), condition=%wide.region_31.32_spmd.clone, body=%wide.region_30.31_spmd.clone.sunk | while | flops 320143360 | bytes 3950711 | solution.py:151
  789.7 23.8 %reduce-scatter.25.cloned.1.call-done = bf16[160,768]{1,0:T(8,128)(2,1)} async-done(((bf16[640,768]{1,0:T(8,128)(2,1)}), bf16[160,768]{1,0:T(8,128)(2,1)}) %reduce-scatter.25.cloned.1.call-update) | async-done | bytes 245776 | tf_op jit(solution)/shard_map/reduce_scatter | solution.py:63
  838.3 86.9 %while.123 = (s32[]{:T(128)}, f32[640,3,64]{0,2,1:T(8,128)S(1)}, f32[7,640,3,64]{1,3,2,0:T(8,128)}, f32[7,640,3,64]{1,3,2,0:T(8,128)}, bf16[7,640,3,64]{1,3,2,0:...) while((s32[]{:T(128)}, f32[640,3,64]{0,2,1:T(8,128)S(1)}, ...), condition=%wide.region_43.44_spmd.clone, body=%wide.region_42.43_spmd.clone.sunk | while | flops 799621120 | bytes 36900012 | solution.py:187
  990.9 23.7 %reduce-scatter.27.cloned.1.call-done = bf16[160,768]{1,0:T(8,128)(2,1)} async-done(((bf16[640,768]{1,0:T(8,128)(2,1)}), bf16[160,768]{1,0:T(8,128)(2,1)}) %reduce-scatter.27.cloned.1.call-update) | async-done | bytes 245776 | tf_op jit(solution)/shard_map/reduce_scatter | solution.py:63
  1027.5 15.3 all_gather.44
  1052.2 27.1 %reduce-scatter.29.cloned.1.call-done = bf16[160,768]{1,0:T(8,128)(2,1)} async-done(((bf16[640,768]{1,0:T(8,128)(2,1)}), bf16[160,768]{1,0:T(8,128)(2,1)}) %reduce-scatter.29.cloned.1.call-update) | async-done | bytes 245776 | tf_op jit(solution)/shard_map/reduce_scatter | solution.py:63
  1102.6 92.3 %while.124 = (s32[]{:T(128)}, f32[640,3,64]{0,2,1:T(8,128)S(1)}, f32[7,640,3,64]{1,3,2,0:T(8,128)}, f32[7,640,3,64]{1,3,2,0:T(8,128)}, bf16[7,640,3,64]{1,3,2,0:...) while((s32[]{:T(128)}, f32[640,3,64]{0,2,1:T(8,128)S(1)}, ...), condition=%wide.region_56.57_spmd.clone, body=%wide.region_55.56_spmd.clone.sunk | while | flops 799621120 | bytes 37883080 | solution.py:187
  1247.9 33.8 %reduce-scatter.31.cloned.1.call-done = bf16[160,768]{1,0:T(8,128)(2,1)} async-done(((bf16[640,768]{1,0:T(8,128)(2,1)}), bf16[160,768]{1,0:T(8,128)(2,1)}) %reduce-scatter.31.cloned.1.call-update) | async-done | bytes 245776 | tf_op jit(solution)/shard_map/reduce_scatter | solution.py:63
  1290.5 15.2 all_gather.46
  1345.8 18.1 %all_gather.47 = bf16[640,768]{1,0:T(8,128)(2,1)S(1)} all-gather(bf16[160,768]{1,0:T(8,128)(2,1)S(1)} %get-tuple-element.1061), channel_id=1, replica_groups=mesh['pipe'=2,'seq'=4,'tensor'=4] {'tensor'}, dimensions={0}, use_global_device_ids=true | all-gather | bytes 1228800 | tf_op jit(solution)/shard_map/all_gather | solution.py:59
  1369.9 91.8 %while.125 = (s32[]{:T(128)}, f32[640,3,64]{0,2,1:T(8,128)S(1)}, f32[7,640,3,64]{1,3,2,0:T(8,128)}, f32[7,640,3,64]{1,3,2,0:T(8,128)}, bf16[7,640,3,64]{1,3,2,0:...) while((s32[]{:T(128)}, f32[640,3,64]{0,2,1:T(8,128)S(1)}, ...), condition=%wide.region_69.70_spmd.clone, body=%wide.region_68.69_spmd.clone.sunk | while | flops 799621120 | bytes 36900012 | solution.py:187
  1530.5 18.4 %all-reduce.1 = (bf16[1,2,192]{2,1,0:T(2,128)(2,1)S(1)}, bf16[1,768]{1,0:T(2,128)(2,1)S(1)}) all-reduce(bf16[1,2,192]{2,1,0:T(2,128)(2,1)S(1)} %fusion.432, bf16[1,768]{1,0:T(2,128)(2,1)S(1)} %broadcast_in_dim.351), channel_id=1, replica_groups=mesh['pipe'=2,'seq'=4,'tensor'=4] {'seq'}, use_global_device_ids=true, to_apply=%region_103.104 | all-reduce | flops 1152 | bytes 4608 | tf_op jit(solution)/shard_map/psum | solution.py:378
  1552.7 77.3 %all-reduce = (f32[1,2,768]{2,1,0:T(2,128)}, f32[1,4,768]{2,1,0:T(4,128)}) all-reduce(f32[1,2,768]{2,1,0:T(2,128)S(1)} %fusion.427, f32[1,4,768]{2,1,0:T(4,128)S(1)} %fusion.424), channel_id=1, replica_groups=mesh['pipe'=2,'seq'=4,'tensor'=4] {'seq','tensor'}, use_global_device_ids=true, to_apply=%region_81.82 | all-reduce | flops 4608 | bytes 36864 | tf_op jit(solution)/shard_map/psum | solution.py:384
  1632.2 56.1 %all-reduce.5.cloned.1.call-done = (bf16[1,768,192]{1,2,0:T(8,128)(2,1)}, bf16[1,2,768,192]{2,3,1,0:T(8,128)(2,1)}, bf16[1,192,768]{2,1,0:T(8,128)(2,1)}, bf16[1...) async-done(((bf16[1,768,192]{1,2,0:T(8,128)(2,1)}, bf16[1,2,768,192]{2,3,1,0:T(8,128)(2,1)}, bf16[1,192,768]{2,1,0:T(8,128)(2,1)}, bf16[1,768,768]{2,1,0:T(8,128)(2,1)}, ...) | async-done | bytes 3538960 | tf_op jit(solution)/shard_map/psum | solution.py:376
  (1372 shorter events, 1267.0 us)
Async XLA Ops:
  7.2 221.5 %reduce-scatter.13.cloned.1.call-start = ((), (), s32[]{:S(2)}) async-start(), calls=%async_computation.12 | async-start | bytes 1228800 | tf_op jit(solution)/shard_map/reduce_scatter | solution.py:63
  59.9 86.2 %collective-permute-start = (bf16[640,192]{0,1:T(8,128)(2,1)S(1)}, bf16[640,192]{0,1:T(8,128)(2,1)S(1)}, u32[]{:S(2)}, u32[]{:S(2)}) collective-permute-start(bf16[640,192]{0,1:T(8,128)(2,1)S(1)} %fusion.234), channel_id=1, source_target_pairs={{0,12},{1,13},{2,14},{3,15},{16,28},{17,29},{18,30},{19,31}} | collective-permute-start | bytes 737288 | tf_op jit(solution)/shard_map/ppermute | solution.py:17
  68.8 78.6 %collective-permute-start.1 = (bf16[640,192]{0,1:T(8,128)(2,1)S(1)}, bf16[640,192]{0,1:T(8,128)(2,1)}, u32[]{:S(2)}, u32[]{:S(2)}) collective-permute-start(bf16[640,192]{0,1:T(8,128)(2,1)S(1)} %fusion.234), channel_id=1, source_target_pairs={{0,8},{4,12},{1,9},{5,13},{2,10},{6,14},{3,11},{7,15},{16,24},{20,... | collective-permute-start | bytes 737288 | tf_op jit(solution)/shard_map/ppermute | solution.py:17
  72.2 76.2 %collective-permute-start.2 = (bf16[640,192]{0,1:T(8,128)(2,1)S(1)}, bf16[640,192]{0,1:T(8,128)(2,1)}, u32[]{:S(2)}, u32[]{:S(2)}) collective-permute-start(bf16[640,192]{0,1:T(8,128)(2,1)S(1)} %fusion.234), channel_id=1, source_target_pairs={{0,4},{4,8},{8,12},{1,5},{5,9},{9,13},{2,6},{6,10},{10,14},{3,7},{... | collective-permute-start | bytes 737288 | tf_op jit(solution)/shard_map/ppermute | solution.py:17
  78.2 71.3 %collective-permute-start.3 = (bf16[640,192]{0,1:T(8,128)(2,1)S(1)}, bf16[640,192]{0,1:T(8,128)(2,1)}, u32[]{:S(2)}, u32[]{:S(2)}) collective-permute-start(bf16[640,192]{0,1:T(8,128)(2,1)S(1)} %fusion.234), channel_id=1, source_target_pairs={{4,0},{8,4},{12,8},{5,1},{9,5},{13,9},{6,2},{10,6},{14,10},{7,3},{... | collective-permute-start | bytes 737288 | tf_op jit(solution)/shard_map/ppermute | solution.py:17
  204.1 77.5 %reduce-scatter.15.cloned.1.call-start = ((), (), s32[]{:S(2)}) async-start(), calls=%async_computation.13 | async-start | bytes 1228800 | tf_op jit(solution)/shard_map/reduce_scatter | solution.py:63
  254.1 254.8 %reduce-scatter.17.cloned.1.call-start = ((), (), s32[]{:S(2)}) async-start(), calls=%async_computation.14 | async-start | bytes 1228800 | tf_op jit(solution)/shard_map/reduce_scatter | solution.py:63
  335.4 83.5 %collective-permute-start.19 = (bf16[640,192]{0,1:T(8,128)(2,1)}, bf16[640,192]{0,1:T(8,128)(2,1)S(1)}, u32[]{:S(2)}, u32[]{:S(2)}) collective-permute-start(bf16[640,192]{0,1:T(8,128)(2,1)} %fusion.236), channel_id=1, source_target_pairs={{0,12},{1,13},{2,14},{3,15},{16,28},{17,29},{18,30},{19,31}} | collective-permute-start | bytes 737288 | tf_op jit(solution)/shard_map/ppermute | solution.py:17
  344.6 76.2 %collective-permute-start.20 = (bf16[640,192]{0,1:T(8,128)(2,1)}, bf16[640,192]{0,1:T(8,128)(2,1)S(1)}, u32[]{:S(2)}, u32[]{:S(2)}) collective-permute-start(bf16[640,192]{0,1:T(8,128)(2,1)} %fusion.236), channel_id=1, source_target_pairs={{0,8},{4,12},{1,9},{5,13},{2,10},{6,14},{3,11},{7,15},{16,24},{20,... | collective-permute-start | bytes 737288 | tf_op jit(solution)/shard_map/ppermute | solution.py:17
  347.0 73.9 %collective-permute-start.21 = (bf16[640,192]{0,1:T(8,128)(2,1)}, bf16[640,192]{0,1:T(8,128)(2,1)}, u32[]{:S(2)}, u32[]{:S(2)}) collective-permute-start(bf16[640,192]{0,1:T(8,128)(2,1)} %fusion.236), channel_id=1, source_target_pairs={{0,4},{4,8},{8,12},{1,5},{5,9},{9,13},{2,6},{6,10},{10,14},{3,7},{... | collective-permute-start | bytes 737288 | tf_op jit(solution)/shard_map/ppermute | solution.py:17
  351.1 71.7 %collective-permute-start.22 = (bf16[640,192]{0,1:T(8,128)(2,1)}, bf16[640,192]{0,1:T(8,128)(2,1)}, u32[]{:S(2)}, u32[]{:S(2)}) collective-permute-start(bf16[640,192]{0,1:T(8,128)(2,1)} %fusion.236), channel_id=1, source_target_pairs={{4,0},{8,4},{12,8},{5,1},{9,5},{13,9},{6,2},{10,6},{14,10},{7,3},{... | collective-permute-start | bytes 737288 | tf_op jit(solution)/shard_map/ppermute | solution.py:17
  353.4 70.4 %collective-permute-start.23 = (bf16[640,192]{0,1:T(8,128)(2,1)}, bf16[640,192]{0,1:T(8,128)(2,1)}, u32[]{:S(2)}, u32[]{:S(2)}) collective-permute-start(bf16[640,192]{0,1:T(8,128)(2,1)} %fusion.236), channel_id=1, source_target_pairs={{8,0},{12,4},{9,1},{13,5},{10,2},{14,6},{11,3},{15,7},{24,16},{28,... | collective-permute-start | bytes 737288 | tf_op jit(solution)/shard_map/ppermute | solution.py:17
  484.2 77.3 %reduce-scatter.19.cloned.1.call-start = ((), (), s32[]{:S(2)}) async-start(), calls=%async_computation.15 | async-start | bytes 1228800 | tf_op jit(solution)/shard_map/reduce_scatter | solution.py:63
  534.1 249.3 %reduce-scatter.21.cloned.1.call-start = ((), (), s32[]{:S(2)}) async-start(), calls=%async_computation.16 | async-start | bytes 1228800 | tf_op jit(solution)/shard_map/reduce_scatter | solution.py:63
  617.6 79.2 %collective-permute-start.38 = (bf16[640,192]{0,1:T(8,128)(2,1)S(1)}, bf16[640,192]{0,1:T(8,128)(2,1)}, u32[]{:S(2)}, u32[]{:S(2)}) collective-permute-start(bf16[640,192]{0,1:T(8,128)(2,1)S(1)} %fusion.238), channel_id=1, source_target_pairs={{0,12},{1,13},{2,14},{3,15},{16,28},{17,29},{18,30},{19,31}} | collective-permute-start | bytes 737288 | tf_op jit(solution)/shard_map/ppermute | solution.py:17
  627.5 71.6 %collective-permute-start.39 = (bf16[640,192]{0,1:T(8,128)(2,1)S(1)}, bf16[640,192]{0,1:T(8,128)(2,1)}, u32[]{:S(2)}, u32[]{:S(2)}) collective-permute-start(bf16[640,192]{0,1:T(8,128)(2,1)S(1)} %fusion.238), channel_id=1, source_target_pairs={{0,8},{4,12},{1,9},{5,13},{2,10},{6,14},{3,11},{7,15},{16,24},{20,... | collective-permute-start | bytes 737288 | tf_op jit(solution)/shard_map/ppermute | solution.py:17
  630.5 69.5 %collective-permute-start.40 = (bf16[640,192]{0,1:T(8,128)(2,1)S(1)}, bf16[640,192]{0,1:T(8,128)(2,1)}, u32[]{:S(2)}, u32[]{:S(2)}) collective-permute-start(bf16[640,192]{0,1:T(8,128)(2,1)S(1)} %fusion.238), channel_id=1, source_target_pairs={{0,4},{4,8},{8,12},{1,5},{5,9},{9,13},{2,6},{6,10},{10,14},{3,7},{... | collective-permute-start | bytes 737288 | tf_op jit(solution)/shard_map/ppermute | solution.py:17
  771.0 243.5 %reduce-scatter.27.cloned.1.call-start = ((), (), s32[]{:S(2)}) async-start(), calls=%async_computation.19 | async-start | bytes 1228800 | tf_op jit(solution)/shard_map/reduce_scatter | solution.py:63
  978.9 100.4 %reduce-scatter.29.cloned.1.call-start = ((), (), s32[]{:S(2)}) async-start(), calls=%async_computation.20 | async-start | bytes 1228800 | tf_op jit(solution)/shard_map/reduce_scatter | solution.py:63
  1051.9 229.8 %reduce-scatter.31.cloned.1.call-start = ((), (), s32[]{:S(2)}) async-start(), calls=%async_computation.21 | async-start | bytes 1228800 | tf_op jit(solution)/shard_map/reduce_scatter | solution.py:63
  1247.8 94.4 %reduce-scatter.33.cloned.1.call-start = ((), (), s32[]{:S(2)}) async-start(), calls=%async_computation.22 | async-start | bytes 1228800 | tf_op jit(solution)/shard_map/reduce_scatter | solution.py:63
  1314.8 212.0 %reduce-scatter.23.cloned.1.call-start = ((), (), s32[]{:S(2)}) async-start(), calls=%async_computation.17 | async-start | bytes 1228800 | tf_op jit(solution)/shard_map/reduce_scatter | solution.py:63
  1325.0 225.1 %reduce-scatter.35.cloned.1.call-start = ((), (), s32[]{:S(2)}) async-start(), calls=%async_computation.23 | async-start | bytes 1228800 | tf_op jit(solution)/shard_map/reduce_scatter | solution.py:63
  1514.2 174.1 %all-reduce.5.cloned.1.call-start = ((), (), s32[]{:S(2)}) async-start(), calls=%async_computation.24 | async-start | bytes 7077888 | tf_op jit(solution)/shard_map/psum | solution.py:376
  (305 other events, 5841.5 us)
Sparse Core Ops, SparseCore 0:
  204.2 24.4 reduce-scatter.12
  254.2 27.2 reduce-scatter.14
  484.3 24.6 reduce-scatter.16
  534.2 27.2 reduce-scatter.18
  758.1 25.2 reduce-scatter.20
  786.2 27.2 reduce-scatter.24
  979.0 35.5 reduce-scatter.26
  1052.0 27.2 reduce-scatter.28
  1247.9 33.6 reduce-scatter.30
  1314.9 27.2 reduce-scatter.32
  1345.2 30.4 reduce-scatter.22
  1514.3 33.7 reduce-scatter.34
  1552.0 136.2 all-reduce.4
where the time goes:
time: 1720 us; the launch traced here: 1700 us
  matrix products  493 us (29%)
  waiting for transfers between devices  328 us (19%)
  blocking collectives  259 us (15%)
  starting transfers between devices  237 us (14%)
  other arithmetic  201 us (12%)
  local copies, waits for them, and re-layouts  164 us (10%)
  between operations  18.2 us (1%)
    ppermute x94, starting transfers between devices, shifted(): return lax.ppermute(block, axis, route)  236 us
    reduce_scatter x12, waiting for transfers between devices, fold_rows(): lax.psum_scatter(partial_sum.astype(jnp.bfloat16), 'tensor', scatter_dime...  210 us
    all_gather x12, blocking collectives, spread_rows(): return lax.all_gather(piece, 'tensor', axis=0, tiled=True)  163 us
    dot_general x42, matrix products, masked_scores(): jnp.einsum('qhd,khd->hqk', query_heads, key_heads, preferred_element_type...  127 us
    dot_general x21, matrix products, second_pass(): jnp.einsum('hqk,khd->qhd', probs, value_heads, preferred_element_type=jnp...  80.5 us
    psum x1, blocking collectives, shards(): vectors = lax.psum((totals['gains'], totals['shifts']), ('seq', 'tensor'))  77.3 us
    reduce_sum x21, other arithmetic, first_pass(): row_sum = row_sum * jnp.exp(row_max - new_max) + jnp.sum(weights, axis=-1)  76.2 us
    ppermute x94, waiting for transfers between devices, shifted(): return lax.ppermute(block, axis, route)  61.8 us
  transfers between devices with their start and end apart: 107, of which 31 were waited for; matrix products, arithmetic and copies ran while one was open for 24% of the time, Pallas kernels for 0%

commit v1 on v0

v1 whole, which is shorter than its diff:
```python
import jax
import jax.numpy as jnp
from jax import lax
from jax.experimental import pallas as pl
from jax.experimental.pallas import tpu as pltpu
from jax.sharding import PartitionSpec as P

HEAD_DIM = 64
REACH = 3
KEY_TILE = 128


EPS = 1e-05
NEG = -1e30


def norm_rows(values_in, gain, shift):
    center = values_in - jnp.mean(values_in, axis=-1, keepdims=True)
    spread = jnp.mean(center * center, axis=-1, keepdims=True)
    return center * lax.rsqrt(spread + EPS) * gain + shift


def gelu_exact(values_in):
    return jax.nn.gelu(values_in, approximate=False)


def matmul(left, right):
    return jnp.dot(left, right, preferred_element_type=jnp.float32)


def inner_rows(left, right):
    return lax.dot_general(
        left, right, (((0,), (0,)), ((), ())), preferred_element_type=jnp.float32
    )


def times_trans(left, right):
    return lax.dot_general(
        left, right, (((1,), (1,)), ((), ())), preferred_element_type=jnp.float32
    )


def spread_rows(piece):
    return lax.all_gather(piece, "tensor", axis=0, tiled=True)


def fold_rows(partial_sum):
    return lax.psum_scatter(
        partial_sum.astype(jnp.bfloat16), "tensor", scatter_dimension=0, tiled=True
    ).astype(jnp.float32)


def swap_cores(block):
    return lax.ppermute(block, "pipe", [(0, 1), (1, 0)])


def shifted(block, distance):
    devices = range(lax.axis_size("seq"))
    route = [(i - distance, i) for i in devices if i - distance in devices]
    return lax.ppermute(block, "seq", route)


def whole_row():
    return lax.axis_size("seq") <= 2 * REACH + 1


def gather_window(block):
    if whole_row():
        return lax.all_gather(block, "seq", axis=0, tiled=True)
    return jnp.concatenate(
        [block if o == 0 else shifted(block, o) for o in range(REACH, -REACH - 1, -1)], axis=0
    )


def return_window(terms):
    if whole_row():
        return lax.psum_scatter(terms, "seq", scatter_dimension=0, tiled=True)
    pieces = jnp.split(terms, 2 * REACH + 1, axis=0)
    total = 0.0
    for piece, offset in zip(pieces, range(REACH, -REACH - 1, -1)):
        got = piece if offset == 0 else shifted(piece, -offset)
        total = total + got.astype(jnp.float32)
    return total.astype(jnp.bfloat16)


def head_parts(matrix, axis):
    head = lax.broadcasted_iota(jnp.int32, matrix.shape, axis) // HEAD_DIM
    return [
        jnp.where(head == h, matrix, 0.0).astype(jnp.bfloat16)
        for h in range(matrix.shape[axis] // HEAD_DIM)
    ]


def attend_kernel(span, keys, values_t, query_t, key_marks, marks, mixed_t, logs, held):
    rows = query_t.shape[1]
    parts = head_parts(query_t[...].astype(jnp.float32) * HEAD_DIM**-0.5, 0)
    held[...] = jnp.zeros_like(held)
    logs[...] = jnp.zeros_like(logs)

    def step(number, carry):
        start = pl.multiple_of(number * KEY_TILE, KEY_TILE)
        key = keys[pl.ds(start, KEY_TILE), :]
        value = values_t[:, pl.ds(start, KEY_TILE)]
        same = key_marks[pl.ds(start, KEY_TILE), :] == marks[...]
        later = []
        for h, part in enumerate(parts):
            top, total = carry[h]
            scores = jnp.where(same, matmul(key, part), NEG)
            new_top = jnp.maximum(top, jnp.max(scores, axis=0, keepdims=True))
            weights = jnp.exp(scores - new_top)
            scale = jnp.exp(top - new_top)
            total = total * scale + jnp.sum(weights, axis=0, keepdims=True)
            own = pl.ds(h * HEAD_DIM, HEAD_DIM)
            held[own, :] = held[own, :] * scale + matmul(
                value[h * HEAD_DIM : (h + 1) * HEAD_DIM, :], weights.astype(jnp.bfloat16)
            )
            later.append((new_top, total))
        return tuple(later)

    first = tuple(
        (jnp.full((1, rows), NEG, jnp.float32), jnp.zeros((1, rows), jnp.float32)) for _ in parts
    )
    last = lax.fori_loop(span[0], span[1], step, first)
    for h, (top, total) in enumerate(last):
        own = pl.ds(h * HEAD_DIM, HEAD_DIM)
        mixed_t[own, :] = (held[own, :] / total).astype(jnp.bfloat16)
        logs[pl.ds(h, 1), :] = top + jnp.log(total)


def attend_back_kernel(
    span, keys, keys_t, values, query, query_t, grad, grad_t, mixed_t, logs, key_marks, marks,
    query_grad_t, key_grad, value_grad, held,
):
    factor = HEAD_DIM**-0.5
    query_parts = head_parts(query[...].astype(jnp.float32) * factor, 1)
    query_t_parts = head_parts(query_t[...].astype(jnp.float32) * factor, 0)
    grad_parts = head_parts(grad[...].astype(jnp.float32), 1)
    grad_t_parts = head_parts(grad_t[...].astype(jnp.float32), 0)
    product = grad_t[...].astype(jnp.float32) * mixed_t[...].astype(jnp.float32)
    deltas = [
        jnp.sum(product[h * HEAD_DIM : (h + 1) * HEAD_DIM, :], axis=0, keepdims=True)
        for h in range(len(query_parts))
    ]
    held[...] = jnp.zeros_like(held)
    key_grad[...] = jnp.zeros_like(key_grad)
    value_grad[...] = jnp.zeros_like(value_grad)

    def step(number, carry):
        start = pl.multiple_of(number * KEY_TILE, KEY_TILE)
        here = pl.ds(start, KEY_TILE)
        key = keys[here, :]
        key_t = keys_t[:, here]
        value = values[here, :]
        same = key_marks[here, :] == marks[...]
        key_total = jnp.zeros(key.shape, jnp.float32)
        value_total = jnp.zeros(key.shape, jnp.float32)
        for h in range(len(query_parts)):
            scores = matmul(key, query_t_parts[h])
            probs = jnp.where(same, jnp.exp(scores - logs[pl.ds(h, 1), :]), 0.0)
            grad_probs = matmul(value, grad_t_parts[h])
            grad_scores = (probs * (grad_probs - deltas[h])).astype(jnp.bfloat16)
            value_total += matmul(probs.astype(jnp.bfloat16), grad_parts[h])
            key_total += matmul(grad_scores, query_parts[h])
            own = pl.ds(h * HEAD_DIM, HEAD_DIM)
            held[own, :] += matmul(key_t[h * HEAD_DIM : (h + 1) * HEAD_DIM, :], grad_scores)
        key_grad[here, :] = key_total.astype(jnp.bfloat16)
        value_grad[here, :] = value_total.astype(jnp.bfloat16)
        return carry

    lax.fori_loop(span[0], span[1], step, 0)
    query_grad_t[...] = (held[...] * factor).astype(jnp.bfloat16)


def vmem(count):
    return [pl.BlockSpec(memory_space=pltpu.SMEM)] + [
        pl.BlockSpec(memory_space=pltpu.VMEM) for _ in range(count)
    ]


def forward_attention(query_t, keys, values_t, clips):
    span, key_marks, marks = clips
    width, rows = query_t.shape
    return pl.pallas_call(
        attend_kernel,
        out_shape=(
            jax.ShapeDtypeStruct((width, rows), jnp.bfloat16),
            jax.ShapeDtypeStruct((8, rows), jnp.float32),
        ),
        in_specs=vmem(5),
        out_specs=tuple(vmem(2)[1:]),
        scratch_shapes=[pltpu.VMEM((width, rows), jnp.float32)],
        compiler_params=pltpu.CompilerParams(vmem_limit_bytes=40 * 2**20),
        name="attend",
    )(span, keys, values_t, query_t, key_marks, marks)


def backward_attention(keys, keys_t, values, query, query_t, grad, grad_t, mixed_t, logs, clips):
    span, key_marks, marks = clips
    width, rows = query_t.shape
    return pl.pallas_call(
        attend_back_kernel,
        out_shape=(
            jax.ShapeDtypeStruct((width, rows), jnp.bfloat16),
            jax.ShapeDtypeStruct(keys.shape, jnp.bfloat16),
            jax.ShapeDtypeStruct(keys.shape, jnp.bfloat16),
        ),
        in_specs=vmem(11),
        out_specs=tuple(vmem(3)[1:]),
        scratch_shapes=[pltpu.VMEM((width, rows), jnp.float32)],
        compiler_params=pltpu.CompilerParams(vmem_limit_bytes=40 * 2**20),
        name="attend_back",
    )(span, keys, keys_t, values, query, query_t, grad, grad_t, mixed_t, logs, key_marks, marks)


def clip_window(clip_here):
    marks = clip_here + 1
    key_marks = gather_window(marks)
    tiles = key_marks.reshape(-1, KEY_TILE)
    hit = jnp.any((tiles >= marks[0]) & (tiles <= marks[-1]), axis=1)
    place = jnp.arange(tiles.shape[0], dtype=jnp.int32)
    low = jnp.min(jnp.where(hit, place, tiles.shape[0]))
    high = jnp.max(jnp.where(hit, place + 1, 0))
    return (jnp.stack([low, high]), key_marks[:, None], marks[None, :])


def layer_forward(layer_in, clips, weights):
    gains, shifts, qkv_w, bias_pair, output_w, expand_w, expand_b, reduce_w = weights
    width = bias_pair.shape[-1]
    resid_in = layer_in.astype(jnp.float32)
    normed = spread_rows(norm_rows(resid_in, gains[0], shifts[0]).astype(jnp.bfloat16))
    no_bias = jnp.zeros((width,), jnp.float32)
    qkv_bias = jnp.concatenate([bias_pair[0], no_bias, bias_pair[1]])
    qkv = (matmul(normed, qkv_w) + qkv_bias).astype(jnp.bfloat16)
    query = qkv[:, :width]
    window = gather_window(qkv[:, width:])
    keys, values = window[:, :width], window[:, width:]
    query_t = query.T
    mixed_t, logs = forward_attention(query_t, keys, values.T, clips)
    resid_mid = resid_in + fold_rows(inner_rows(mixed_t, output_w)) + shifts[2]
    normed_mid = spread_rows(norm_rows(resid_mid, gains[1], shifts[1]).astype(jnp.bfloat16))
    expanded = matmul(normed_mid, expand_w) + expand_b
    activated = gelu_exact(expanded).astype(jnp.bfloat16)
    layer_out = (resid_mid + fold_rows(matmul(activated, reduce_w)) + shifts[3]).astype(
        jnp.bfloat16
    )
    saved = (
        layer_in, normed, query, query_t, keys, values, mixed_t, logs, resid_mid, normed_mid,
        expanded, activated,
    )
    return (layer_out, saved)


def layer_backward(layer_grad, saved, clips, weights):
    gains, shifts, qkv_w, bias_pair, output_w, expand_w, expand_b, reduce_w = weights
    (
        layer_in, normed, query, query_t, keys, values, mixed_t, logs, resid_mid, normed_mid,
        expanded, activated,
    ) = saved
    grad_out = layer_grad.astype(jnp.float32)
    grad_all = spread_rows(layer_grad)
    grad_act = times_trans(grad_all, reduce_w)
    gelu_back = jax.vjp(gelu_exact, expanded)[1]
    grad_expanded = gelu_back(grad_act)[0].astype(jnp.bfloat16)
    grad_normed_mid = fold_rows(times_trans(grad_expanded, expand_w))
    grad_reduce = inner_rows(activated, grad_all).astype(jnp.bfloat16)
    grad_expand_bias = jnp.sum(grad_expanded, axis=0, dtype=jnp.float32)
    grad_expand = inner_rows(normed_mid, grad_expanded).astype(jnp.bfloat16)
    feed_sum = sum_half(grad_expand, grad_reduce)
    mid_back = jax.vjp(norm_rows, resid_mid, gains[1], shifts[1])[1]
    grad_mid_norm, grad_gain_mid, grad_shift_mid = mid_back(grad_normed_mid)
    grad_mid = grad_out + grad_mid_norm
    grad_branch = spread_rows(grad_mid.astype(jnp.bfloat16))
    grad_mixed = times_trans(grad_branch, output_w).astype(jnp.bfloat16)
    query_grad_t, key_terms, value_terms = backward_attention(
        keys, keys.T, values, query, query_t, grad_mixed, grad_mixed.T, mixed_t, logs, clips
    )
    grad_output = matmul(mixed_t, grad_branch).astype(jnp.bfloat16)
    grad_keyval = return_window(jnp.concatenate([key_terms, value_terms], axis=1))
    grad_qkv = jnp.concatenate([query_grad_t.T, grad_keyval], axis=1)
    grad_normed = fold_rows(times_trans(grad_qkv, qkv_w))
    grad_qkv_w = inner_rows(normed, grad_qkv).astype(jnp.bfloat16)
    half = grad_qkv_w.shape[0] // 2
    half_out = grad_output.shape[0] // 2
    qkv_sum = sum_half(grad_qkv_w[:half], grad_qkv_w[half:])
    output_sum = sum_half(grad_output[:half_out], grad_output[half_out:])
    qkv_bias = jnp.sum(grad_qkv, axis=0, dtype=jnp.float32)
    in_back = jax.vjp(norm_rows, layer_in.astype(jnp.float32), gains[0], shifts[0])[1]
    grad_in_norm, grad_gain_in, grad_shift_in = in_back(grad_normed)
    input_grad = (grad_mid + grad_in_norm).astype(jnp.bfloat16)
    norms = jnp.stack(
        [
            grad_gain_in, grad_gain_mid, grad_shift_in, grad_shift_mid,
            jnp.sum(grad_mid, axis=0), jnp.sum(grad_out, axis=0),
        ]
    )
    biases = jnp.concatenate([qkv_bias, grad_expand_bias])
    return (input_grad, (feed_sum, qkv_sum, output_sum), norms, biases)


def sum_half(first, second):
    core = lax.axis_index("pipe") == 0
    kept = jnp.where(core, first, second)
    got = swap_cores(jnp.where(core, second, first))
    return lax.psum(kept + got, "seq")


def shards(
    frames,
    clip_ids,
    cotangent,
    norm_gains,
    norm_shifts,
    query_projection_weight,
    w_keyval,
    proj_bias,
    w_output,
    w_expand,
    expand_bias,
    w_reduce,
):
    core = lax.axis_index("pipe")
    low_core = core == 0
    qkv_w = jnp.concatenate([query_projection_weight[0], w_keyval[0, 0], w_keyval[0, 1]], axis=1)
    own = (
        norm_gains[0], norm_shifts[0], qkv_w, proj_bias[0], w_output[0], w_expand[0],
        expand_bias[0], w_reduce[0],
    )
    other = tuple(swap_cores(item) for item in own)
    weights = [
        tuple(jnp.where(low_core, a, b) for a, b in zip(own, other)),
        tuple(jnp.where(low_core, b, a) for a, b in zip(own, other)),
    ]
    clips = clip_window(lax.dynamic_index_in_dim(clip_ids, core, 0, keepdims=False))
    stream = lax.dynamic_index_in_dim(frames, core, 0, keepdims=False)
    outs, saved = [], []
    for number in range(2):
        stream, kept = layer_forward(stream, clips, weights[number])
        outs.append(stream)
        saved.append(kept)
    grad = lax.dynamic_index_in_dim(cotangent, core, 0, keepdims=False)
    grads, sums, norms, biases = [None] * 2, [None] * 2, [None] * 2, [None] * 2
    for number in (1, 0):
        grad, sums[number], norms[number], biases[number] = layer_backward(
            grad, saved[number], clips, weights[number]
        )
        grads[number] = grad

    def both_batches(pair):
        mine = jnp.where(low_core, pair[0], pair[1])
        got = swap_cores(jnp.where(low_core, pair[1], pair[0]))
        return jnp.stack([jnp.where(low_core, mine, got), jnp.where(low_core, got, mine)])[None]

    def both_halves(place):
        mine = jnp.where(low_core, sums[0][place], sums[1][place])
        got = swap_cores(jnp.where(low_core, sums[1][place], sums[0][place]))
        return (
            jnp.where(low_core, mine, got).astype(jnp.float32),
            jnp.where(low_core, got, mine).astype(jnp.float32),
        )

    states = both_batches(outs)
    input_grads = both_batches(grads)
    grad_expand, grad_reduce = both_halves(0)
    grad_qkv = jnp.concatenate(both_halves(1), axis=0)
    grad_output = jnp.concatenate(both_halves(2), axis=0)
    norm_sum = lax.psum(jnp.stack(norms), ("pipe", "seq", "tensor"))
    norm_sum = lax.dynamic_index_in_dim(norm_sum, core, 0, keepdims=False)
    bias_sum = lax.psum(jnp.stack(biases), ("pipe", "seq"))
    bias_sum = lax.dynamic_index_in_dim(bias_sum, core, 0, keepdims=False)
    width = proj_bias.shape[-1]
    return (
        states,
        input_grads,
        norm_sum[None, :2],
        norm_sum[None, 2:],
        grad_qkv[None, :, :width],
        jnp.stack([grad_qkv[:, width : 2 * width], grad_qkv[:, 2 * width :]])[None],
        jnp.stack([bias_sum[:width], bias_sum[2 * width : 3 * width]])[None],
        grad_output[None],
        grad_expand[None],
        bias_sum[None, 3 * width :],
        grad_reduce[None],
    )


def solution(mesh):
    return jax.shard_map(
        shards,
        mesh=mesh,
        in_specs=(
            P(None, ("seq", "tensor"), None),
            P(None, "seq"),
            P(None, ("seq", "tensor"), None),
            P("pipe", None, None),
            P("pipe", None, None),
            P("pipe", None, "tensor"),
            P("pipe", None, None, "tensor"),
            P("pipe", None, "tensor"),
            P("pipe", "tensor", None),
            P("pipe", None, "tensor"),
            P("pipe", "tensor"),
            P("pipe", "tensor", None),
        ),
        out_specs=(
            P("pipe", None, ("seq", "tensor"), None),
            P("pipe", None, ("seq", "tensor"), None),
            P("pipe", None, None),
            P("pipe", None, None),
            P("pipe", None, "tensor"),
            P("pipe", None, None, "tensor"),
            P("pipe", None, "tensor"),
            P("pipe", "tensor", None),
            P("pipe", None, "tensor"),
            P("pipe", "tensor"),
            P("pipe", "tensor", None),
        ),
        check_vma=False,
    )
```

time: 1720 us -> 855 us (0.50)
  matrix products: 493 us -> 61.2 us
  starting transfers between devices: 237 us -> 12.9 us
  other arithmetic: 201 us -> 61.4 us
  local copies, waits for them, and re-layouts: 164 us -> 66.5 us
  blocking collectives: 259 us -> 199 us
  Pallas kernels: 0 us -> 58.6 us
  waiting for transfers between devices: 328 us -> 373 us
    dot_general x147 -> x0, matrix products: 391 us -> none  [the longest x42 127 us: masked_scores(): jnp.einsum('qhd,khd->hqk', query_heads, key_heads, preferred_element_type...]
    ppermute x94 -> x19, starting transfers between devices: 236 us -> 11.8 us  [swap_cores(): return lax.ppermute(block, 'pipe', [(0, 1), (1, 0)])]
    reduce_sum x30 -> x2, other arithmetic: 82 us -> 1.65 us  [layer_backward(): qkv_bias = jnp.sum(grad_qkv, axis=0, dtype=jnp.float32)]
    all_gather x0 -> x2, waiting for transfers between devices: none -> 67.7 us  [gather_window(): return lax.all_gather(block, 'seq', axis=0, tiled=True)]
    reduce_scatter x0 -> x2, waiting for transfers between devices: none -> 65.6 us  [return_window(): return lax.psum_scatter(terms, 'seq', scatter_dimension=0, tiled=True)]
    ppermute x94 -> x19, waiting for transfers between devices: 61.8 us -> 1.81 us  [swap_cores(): return lax.ppermute(block, 'pipe', [(0, 1), (1, 0)])]
    dynamic_slice x105 -> x0, local copies, waits for them, and re-layouts: 59.7 us -> none  [forward_attention(): lax.scan(first_pass, (start_max, start_sum), (key_blocks, marks_win))]
    pallas_call x0 -> x4, Pallas kernels: none -> 58.6 us  [the longest x2 31.9 us: backward_attention(): pl.pallas_call(attend_back_kernel, out_shape=(jax.ShapeDtypeStruct((width...]
  transfers between devices with their start and end apart: 107 -> 32, of which waited for: 31 -> 14; matrix products, arithmetic and copies ran while one was open for 24% -> 10% of each run, Pallas kernels for 0% -> 2%
where the time goes in v1:
time: 855 us; the launch traced here: 848 us
  waiting for transfers between devices  373 us (44%)
  blocking collectives  199 us (23%)
  local copies, waits for them, and re-layouts  66.5 us (8%)
  other arithmetic  61.4 us (7%)
  matrix products  61.2 us (7%)
  Pallas kernels  58.6 us (7%)
  between operations  15.3 us (2%)
  starting transfers between devices  12.9 us (2%)
    reduce_scatter x8, waiting for transfers between devices, fold_rows(): lax.psum_scatter(partial_sum.astype(jnp.bfloat16), 'tensor', scatter_dime...  154 us
    all_gather x8, blocking collectives, spread_rows(): return lax.all_gather(piece, 'tensor', axis=0, tiled=True)  113 us
    psum x1, waiting for transfers between devices, sum_half(): return lax.psum(kept + got, 'seq')  84 us
    all_gather x2, waiting for transfers between devices, gather_window(): return lax.all_gather(block, 'seq', axis=0, tiled=True)  67.7 us
    reduce_scatter x2, waiting for transfers between devices, return_window(): return lax.psum_scatter(terms, 'seq', scatter_dimension=0, tiled=True)  65.6 us
    psum x1, blocking collectives, shards(): norm_sum = lax.psum(jnp.stack(norms), ('pipe', 'seq', 'tensor'))  43.2 us
    pallas_call x2, Pallas kernels, backward_attention(): pl.pallas_call(attend_back_kernel, out_shape=(jax.ShapeDtypeStruct((width...  31.9 us
    unnamed x184, local copies, waits for them, and re-layouts  31.9 us
  transfers between devices with their start and end apart: 32, of which 14 were waited for; matrix products, arithmetic and copies ran while one was open for 10% of the time, Pallas kernels for 2%

profile of v1, /device:TPU:0, one launch (start us, length us, event | category | flops | bytes accessed | tf_op | source)
XLA Modules:
  0.0 847.7 jit_solution(8861276710061352451)
XLA Ops:
  11.6 14.9 %all_gather.34 = bf16[640,768]{1,0:T(8,128)(2,1)S(1)} all-gather(bf16[160,768]{1,0:T(8,128)(2,1)S(1)} %fusion.38), channel_id=1, replica_groups=mesh['pipe'=2,'seq'=4,'tensor'=4] {'tensor'}, dimensions={0}, use_global_device_ids=true | all-gather | bytes 1228800 | tf_op jit(solution)/shard_map/all_gather | solution.py:44
  29.9 13.4 %all-gather = s32[1,2560]{1,0:T(1,128)S(1)} all-gather(s32[1,640]{1,0:T(1,128)S(1)} %dynamic-slice_add_fusion.marks), channel_id=2, replica_groups=mesh['pipe'=2,'seq'=4,'tensor'=4] {'seq'}, dimensions={1}, use_global_device_ids=true | all-gather | bytes 12800 | tf_op jit(solution)/shard_map/all_gather | solution.py:69
  48.5 25.5 %all-gather.5.cloned.1.call-done = bf16[2560,384]{0,1:T(8,128)(2,1)} async-done(((bf16[640,384]{0,1:T(8,128)(2,1)}), bf16[2560,384]{0,1:T(8,128)(2,1)}) %all-gather.5.cloned.1.call-update) | async-done | bytes 1966096 | tf_op jit(solution)/shard_map/all_gather | solution.py:69
  80.3 13.3 %attend.2 = (bf16[192,640]{1,0:T(8,128)(2,1)S(1)}, f32[8,640]{1,0:T(8,128)S(1)}) custom-call(s32[2]{0:T(128)S(1)} %pad_add_fusion.span, bf16[2560,192]{1,0:T(8,128)(2,1)S(1)} %copy.35.keys, bf16[192,2560]{1,0:T(8,128)(2,1)S(1)} %copy-done.6, bf16[192,640]{1,0:T(8,128)(2,1)S(1)} %get-tuple-element.103.query_t, s32[2560,1]{1,0:T(8,128)S(1)} %copy.36.key_marks, ...), custom_call_target="tpu_custom_call" | custom-call | tf_op jit(solution)/shard_map/attend/pallas_call | solution.py:183
  99.5 26.3 %reduce-scatter.11.cloned.1.call-done = bf16[160,768]{1,0:T(8,128)(2,1)} async-done(((bf16[640,768]{1,0:T(8,128)(2,1)}), bf16[160,768]{1,0:T(8,128)(2,1)}) %reduce-scatter.11.cloned.1.call-update) | async-done | bytes 245776 | tf_op jit(solution)/shard_map/reduce_scatter | solution.py:48
  129.7 12.9 %all_gather.36 = bf16[640,768]{1,0:T(8,128)(2,1)S(1)} all-gather(bf16[160,768]{1,0:T(8,128)(2,1)S(1)} %add_convert_fusion.9), channel_id=1, replica_groups=mesh['pipe'=2,'seq'=4,'tensor'=4] {'tensor'}, dimensions={0}, use_global_device_ids=true | all-gather | bytes 1228800 | tf_op jit(solution)/shard_map/all_gather | solution.py:44
  152.1 28.2 %reduce-scatter.13.cloned.1.call-done = bf16[160,768]{1,0:T(8,128)(2,1)} async-done(((bf16[640,768]{1,0:T(8,128)(2,1)}), bf16[160,768]{1,0:T(8,128)(2,1)}) %reduce-scatter.13.cloned.1.call-update) | async-done | bytes 245776 | tf_op jit(solution)/shard_map/reduce_scatter | solution.py:48
  182.6 12.9 %all_gather.37 = bf16[640,768]{1,0:T(8,128)(2,1)S(1)} all-gather(bf16[160,768]{1,0:T(8,128)(2,1)S(1)} %fusion.36), channel_id=1, replica_groups=mesh['pipe'=2,'seq'=4,'tensor'=4] {'tensor'}, dimensions={0}, use_global_device_ids=true | all-gather | bytes 1228800 | tf_op jit(solution)/shard_map/all_gather | solution.py:44
  201.5 42.1 %all-gather.7.cloned.1.call-done = bf16[2560,384]{0,1:T(8,128)(2,1)} async-done(((bf16[640,384]{0,1:T(8,128)(2,1)}), bf16[2560,384]{0,1:T(8,128)(2,1)}) %all-gather.7.cloned.1.call-update) | async-done | bytes 1966096 | tf_op jit(solution)/shard_map/all_gather | solution.py:69
  253.0 13.4 %attend.3 = (bf16[192,640]{1,0:T(8,128)(2,1)S(1)}, f32[8,640]{1,0:T(8,128)S(1)}) custom-call(s32[2]{0:T(128)S(1)} %pad_add_fusion.span, bf16[2560,192]{1,0:T(8,128)(2,1)S(1)} %copy-done, bf16[192,2560]{1,0:T(8,128)(2,1)S(1)} %copy-done.7, bf16[192,640]{1,0:T(8,128)(2,1)S(1)} %copy-done.8, s32[2560,1]{1,0:T(8,128)S(1)} %copy.36.key_marks, ...), custom_call_target="tpu_custom_call" | custom-call | tf_op jit(solution)/shard_map/attend/pallas_call | solution.py:183
  270.6 20.9 %all-gather.1 = bf16[1,640,768]{2,1,0:T(8,128)(2,1)} all-gather(bf16[1,160,768]{2,1,0:T(8,128)(2,1)S(1)} %get-tuple-element.72), channel_id=3, replica_groups=mesh['pipe'=2,'seq'=4,'tensor'=4] {'tensor'}, dimensions={1}, use_global_device_ids=true | all-gather | bytes 1228800 | tf_op jit(solution)/shard_map/all_gather | solution.py:44
  336.4 23.1 %reduce-scatter.19.cloned.1.call-done = bf16[160,768]{1,0:T(8,128)(2,1)} async-done(((bf16[640,768]{1,0:T(8,128)(2,1)}), bf16[160,768]{1,0:T(8,128)(2,1)}) %reduce-scatter.19.cloned.1.call-update) | async-done | bytes 245776 | tf_op jit(solution)/shard_map/reduce_scatter | solution.py:48
  365.1 12.9 %all_gather.41 = bf16[640,768]{1,0:T(8,128)(2,1)S(1)} all-gather(bf16[160,768]{1,0:T(8,128)(2,1)S(1)} %convert_element_type.190), channel_id=1, replica_groups=mesh['pipe'=2,'seq'=4,'tensor'=4] {'tensor'}, dimensions={0}, use_global_device_ids=true | all-gather | bytes 1228800 | tf_op jit(solution)/shard_map/all_gather | solution.py:44
  390.6 15.9 %attend_back.2 = (bf16[192,640]{1,0:T(8,128)(2,1)S(1)}, bf16[2560,192]{1,0:T(8,128)(2,1)S(1)}, bf16[2560,192]{1,0:T(8,128)(2,1)S(1)}) custom-call(s32[2]{0:T(128)S(1)} %pad_add_fusion.span, bf16[2560,192]{1,0:T(8,128)(2,1)S(1)} %copy-done.1, bf16[192,2560]{1,0:T(8,128)(2,1)S(1)} %copy-done.5, bf16[2560,192]{1,0:T(8,128)(2,1)S(1)} %copy-done.3, ...), custom_call_target="tpu_custom_call" | custom-call | tf_op jit(solution)/shard_map/attend_back/pallas_call | solution.py:200
  411.6 43.7 %reduce-scatter.21.cloned.1.call-done = bf16[640,384]{1,0:T(8,128)(2,1)} async-done(((bf16[2560,384]{1,0:T(8,128)(2,1)}), bf16[640,384]{1,0:T(8,128)(2,1)}) %reduce-scatter.21.cloned.1.call-update) | async-done | bytes 491536 | tf_op jit(solution)/shard_map/reduce_scatter | solution.py:77
  459.0 26.6 %reduce-scatter.23.cloned.1.call-done = bf16[160,768]{1,0:T(8,128)(2,1)} async-done(((bf16[640,768]{1,0:T(8,128)(2,1)}), bf16[160,768]{1,0:T(8,128)(2,1)}) %reduce-scatter.23.cloned.1.call-update) | async-done | bytes 245776 | tf_op jit(solution)/shard_map/reduce_scatter | solution.py:48
  514.4 23.2 %reduce-scatter.25.cloned.1.call-done = bf16[160,768]{1,0:T(8,128)(2,1)} async-done(((bf16[640,768]{1,0:T(8,128)(2,1)}), bf16[160,768]{1,0:T(8,128)(2,1)}) %reduce-scatter.25.cloned.1.call-update) | async-done | bytes 245776 | tf_op jit(solution)/shard_map/reduce_scatter | solution.py:48
  543.1 12.9 %all_gather.43 = bf16[640,768]{1,0:T(8,128)(2,1)S(1)} all-gather(bf16[160,768]{1,0:T(8,128)(2,1)S(1)} %convert_element_type.200), channel_id=1, replica_groups=mesh['pipe'=2,'seq'=4,'tensor'=4] {'tensor'}, dimensions={0}, use_global_device_ids=true | all-gather | bytes 1228800 | tf_op jit(solution)/shard_map/all_gather | solution.py:44
  565.4 16.0 %attend_back.3 = (bf16[192,640]{1,0:T(8,128)(2,1)S(1)}, bf16[2560,192]{1,0:T(8,128)(2,1)S(1)}, bf16[2560,192]{1,0:T(8,128)(2,1)S(1)}) custom-call(s32[2]{0:T(128)S(1)} %pad_add_fusion.span, bf16[2560,192]{1,0:T(8,128)(2,1)S(1)} %copy.35.keys, bf16[192,2560]{1,0:T(8,128)(2,1)S(1)} %copy-done.4, bf16[2560,192]{1,0:T(8,128)(2,1)S(1)} %copy-done.2, ...), custom_call_target="tpu_custom_call" | custom-call | tf_op jit(solution)/shard_map/attend_back/pallas_call | solution.py:200
  608.4 21.9 %reduce-scatter.27.cloned.1.call-done = bf16[640,384]{1,0:T(8,128)(2,1)} async-done(((bf16[2560,384]{1,0:T(8,128)(2,1)}), bf16[640,384]{1,0:T(8,128)(2,1)}) %reduce-scatter.27.cloned.1.call-update) | async-done | bytes 491536 | tf_op jit(solution)/shard_map/reduce_scatter | solution.py:77
  642.6 17.1 %reduce-scatter.17.cloned.1.call-done = bf16[160,768]{1,0:T(8,128)(2,1)} async-done(((bf16[640,768]{1,0:T(8,128)(2,1)}), bf16[160,768]{1,0:T(8,128)(2,1)}) %reduce-scatter.17.cloned.1.call-update) | async-done | bytes 245776 | tf_op jit(solution)/shard_map/reduce_scatter | solution.py:48
  666.3 29.0 %psum.59 = f32[2,1344]{1,0:T(2,128)S(1)} all-reduce(f32[2,1344]{1,0:T(2,128)S(1)} %pad_maximum_fusion.10), channel_id=1, replica_groups=mesh['pipe'=2,'seq'=4,'tensor'=4] {'pipe','seq'}, use_global_device_ids=true, to_apply=%region_48.49 | all-reduce | flops 2688 | bytes 21504 | tf_op jit(solution)/shard_map/psum | solution.py:368
  701.1 43.2 %psum.56 = f32[2,6,768]{2,1,0:T(8,128)S(1)} all-reduce(f32[2,6,768]{2,1,0:T(8,128)S(1)} %pad_maximum_fusion.9), channel_id=1, replica_groups=mesh['pipe'=2,'seq'=4,'tensor'=4] {'pipe','seq','tensor'}, use_global_device_ids=true, to_apply=%region_41.42 | all-reduce | flops 9216 | bytes 73728 | tf_op jit(solution)/shard_map/psum | solution.py:366
  746.3 84.0 %all-reduce.3.cloned.1.call-done = (bf16[384,576]{0,1:T(8,128)(2,1)}, bf16[384,576]{0,1:T(8,128)(2,1)}, bf16[96,768]{1,0:T(8,128)(2,1)}, bf16[96,768]{1,0:T(8,12...) async-done(((bf16[384,576]{0,1:T(8,128)(2,1)}, bf16[384,576]{0,1:T(8,128)(2,1)}, bf16[96,768]{1,0:T(8,128)(2,1)}, bf16[96,768]{1,0:T(8,128)(2,1)}, ...) | async-done | bytes 3538960 | tf_op jit(solution)/shard_map/psum | solution.py:304
  (411 shorter events, 239.0 us)
Async XLA Ops:
  7.2 66.8 %all-gather.5.cloned.1.call-start = ((), (), s32[]{:S(2)}) async-start(), calls=%async_computation.10 | async-start | bytes 2457600 | tf_op jit(solution)/shard_map/all_gather | solution.py:69
  10.6 15.9 %collective-permute-start.2 = (bf16[768,576]{0,1:T(8,128)(2,1)S(1)}, bf16[768,576]{0,1:T(8,128)(2,1)}, u32[]{:S(2)}, u32[]{:S(2)}) collective-permute-start(bf16[768,576]{0,1:T(8,128)(2,1)S(1)} %pad_maximum_fusion.2), channel_id=1, source_target_pairs={{0,16},{16,0},{1,17},{17,1},{2,18},{18,2},{3,19},{19,3},{4,20},{20... | collective-permute-start | bytes 2654216 | tf_op jit(solution)/shard_map/ppermute | solution.py:54
  29.7 96.2 %reduce-scatter.11.cloned.1.call-start = ((), (), s32[]{:S(2)}) async-start(), calls=%async_computation.11 | async-start | bytes 1228800 | tf_op jit(solution)/shard_map/reduce_scatter | solution.py:48
  29.8 63.9 %collective-permute-start.4 = (bf16[192,768]{1,0:T(8,128)(2,1)S(1)}, bf16[192,768]{1,0:T(8,128)(2,1)}, u32[]{:S(2)}, u32[]{:S(2)}) collective-permute-start(bf16[192,768]{1,0:T(8,128)(2,1)S(1)} %bitcast.242), channel_id=1, source_target_pairs={{0,16},{16,0},{1,17},{17,1},{2,18},{18,2},{3,19},{19,3},{4,20},{20... | collective-permute-start | bytes 884744 | tf_op jit(solution)/shard_map/ppermute | solution.py:54
  95.1 85.1 %reduce-scatter.13.cloned.1.call-start = ((), (), s32[]{:S(2)}) async-start(), calls=%async_computation.12 | async-start | bytes 1228800 | tf_op jit(solution)/shard_map/reduce_scatter | solution.py:48
  98.7 50.3 %collective-permute-start.7 = (bf16[768,768]{1,0:T(8,128)(2,1)}, bf16[768,768]{1,0:T(8,128)(2,1)}, u32[]{:S(2)}, u32[]{:S(2)}) collective-permute-start(bf16[768,768]{1,0:T(8,128)(2,1)} %bitcast.259), channel_id=1, source_target_pairs={{0,16},{16,0},{1,17},{17,1},{2,18},{18,2},{3,19},{19,3},{4,20},{20... | collective-permute-start | bytes 3538952 | tf_op jit(solution)/shard_map/ppermute | solution.py:54
  98.8 43.8 %collective-permute-start.5 = (bf16[768,768]{1,0:T(8,128)(2,1)}, bf16[768,768]{1,0:T(8,128)(2,1)}, u32[]{:S(2)}, u32[]{:S(2)}) collective-permute-start(bf16[768,768]{1,0:T(8,128)(2,1)} %bitcast.258), channel_id=1, source_target_pairs={{0,16},{16,0},{1,17},{17,1},{2,18},{18,2},{3,19},{19,3},{4,20},{20... | collective-permute-start | bytes 3538952 | tf_op jit(solution)/shard_map/ppermute | solution.py:54
  151.9 91.6 %all-gather.7.cloned.1.call-start = ((), (), s32[]{:S(2)}) async-start(), calls=%async_computation.13 | async-start | bytes 2457600 | tf_op jit(solution)/shard_map/all_gather | solution.py:69
  199.6 101.0 %reduce-scatter.15.cloned.1.call-start = ((), (), s32[]{:S(2)}) async-start(), calls=%async_computation.14 | async-start | bytes 1228800 | tf_op jit(solution)/shard_map/reduce_scatter | solution.py:48
  268.8 90.7 %reduce-scatter.19.cloned.1.call-start = ((), (), s32[]{:S(2)}) async-start(), calls=%async_computation.16 | async-start | bytes 1228800 | tf_op jit(solution)/shard_map/reduce_scatter | solution.py:48
  332.1 123.1 %reduce-scatter.21.cloned.1.call-start = ((), (), s32[]{:S(2)}) async-start(), calls=%async_computation.17 | async-start | bytes 2457600 | tf_op jit(solution)/shard_map/reduce_scatter | solution.py:77
  409.3 76.3 %reduce-scatter.23.cloned.1.call-start = ((), (), s32[]{:S(2)}) async-start(), calls=%async_computation.18 | async-start | bytes 1228800 | tf_op jit(solution)/shard_map/reduce_scatter | solution.py:48
  459.0 78.6 %reduce-scatter.25.cloned.1.call-start = ((), (), s32[]{:S(2)}) async-start(), calls=%async_computation.19 | async-start | bytes 1228800 | tf_op jit(solution)/shard_map/reduce_scatter | solution.py:48
  510.2 120.1 %reduce-scatter.27.cloned.1.call-start = ((), (), s32[]{:S(2)}) async-start(), calls=%async_computation.20 | async-start | bytes 2457600 | tf_op jit(solution)/shard_map/reduce_scatter | solution.py:77
  584.1 75.6 %reduce-scatter.17.cloned.1.call-start = ((), (), s32[]{:S(2)}) async-start(), calls=%async_computation.15 | async-start | bytes 1228800 | tf_op jit(solution)/shard_map/reduce_scatter | solution.py:48
  590.3 6.5 collective-permute-start.17
  596.1 100.6 %reduce-scatter.29.cloned.1.call-start = ((), (), s32[]{:S(2)}) async-start(), calls=%async_computation.21 | async-start | bytes 1228800 | tf_op jit(solution)/shard_map/reduce_scatter | solution.py:48
  603.6 29.8 %collective-permute-start.11 = (bf16[384,576]{0,1:T(8,128)(2,1)}, bf16[384,576]{0,1:T(8,128)(2,1)}, u32[]{:S(2)}, u32[]{:S(2)}) collective-permute-start(bf16[384,576]{0,1:T(8,128)(2,1)} %broadcast_select_fusion.24), channel_id=1, source_target_pairs={{0,16},{16,0},{1,17},{17,1},{2,18},{18,2},{3,19},{19,3},{4,20},{20... | collective-permute-start | bytes 1327112 | tf_op jit(solution)/shard_map/ppermute | solution.py:54
  607.9 30.0 %collective-permute-start.16 = (bf16[768,768]{1,0:T(8,128)(2,1)}, bf16[768,768]{1,0:T(8,128)(2,1)}, u32[]{:S(2)}, u32[]{:S(2)}) collective-permute-start(bf16[768,768]{1,0:T(8,128)(2,1)} %get-tuple-element.132), channel_id=1, source_target_pairs={{0,16},{16,0},{1,17},{17,1},{2,18},{18,2},{3,19},{19,3},{4,20},{20... | collective-permute-start | bytes 3538952 | tf_op jit(solution)/shard_map/ppermute | solution.py:54
  633.3 197.0 %all-reduce.3.cloned.1.call-start = ((), (), s32[]{:S(2)}) async-start(), calls=%async_computation.22 | async-start | bytes 7077888 | tf_op jit(solution)/shard_map/psum | solution.py:304
  635.9 5.2 collective-permute-start.13
  637.3 4.4 collective-permute-start.10
  700.6 44.9 %collective-permute-start.9 = (bf16[160,768]{1,0:T(8,128)(2,1)S(1)}, bf16[160,768]{1,0:T(8,128)(2,1)S(1)}, u32[]{:S(2)}, u32[]{:S(2)}) collective-permute-start(bf16[160,768]{1,0:T(8,128)(2,1)S(1)} %get-tuple-element.75), channel_id=1, source_target_pairs={{0,16},{16,0},{1,17},{17,1},{2,18},{18,2},{3,19},{19,3},{4,20},{20... | collective-permute-start | bytes 737288 | tf_op jit(solution)/shard_map/ppermute | solution.py:54
  833.3 4.6 collective-permute-start.18
  (100 other events, 617.8 us)
Sparse Core Ops, SparseCore 0:
  29.8 44.1 all-gather.4
  95.3 30.5 reduce-scatter.10
  152.1 28.1 reduce-scatter.12
  199.8 43.7 all-gather.6
  269.0 31.6 reduce-scatter.14
  332.3 27.2 reduce-scatter.18
  409.4 45.8 reduce-scatter.20
  459.1 26.4 reduce-scatter.22
  510.3 27.2 reduce-scatter.24
  584.3 45.9 reduce-scatter.26
  633.2 26.4 reduce-scatter.16
  662.5 27.2 reduce-scatter.28
  693.8 136.5 all-reduce.2

commit v2 on v1

--- a/solution.py
+++ b/solution.py
@@ -1,3 +1,5 @@
+import functools
+
 import jax
 import jax.numpy as jnp
 from jax import lax
@@ -40,14 +42,111 @@
     )
 
 
+def meet(axis):
+    count = lax.axis_size(axis)
+    me = lax.axis_index(axis)
+    peers = [lax.rem(me + step, count) for step in range(1, count)]
+    barrier = pltpu.get_barrier_semaphore()
+    for peer in peers:
+        pl.semaphore_signal(
+            barrier, inc=1, device_id={axis: peer}, device_id_type=pl.DeviceIdType.MESH
+        )
+    pl.semaphore_wait(barrier, count - 1)
+    return (me, peers)
+
+
+def push(source, target, sent, landed, axis, peer):
+    copy = pltpu.make_async_remote_copy(
+        src_ref=source,
+        dst_ref=target,
+        send_sem=sent,
+        recv_sem=landed,
+        device_id={axis: peer},
+        device_id_type=pl.DeviceIdType.MESH,
+    )
+    copy.start()
+    return copy
+
+
+def spread_kernel(piece, whole, sent, landed):
+    me, peers = meet("tensor")
+    rows = piece.shape[0]
+    own = pl.ds(pl.multiple_of(me * rows, rows), rows)
+    copies = [
+        push(piece, whole.at[own], sent.at[k], landed.at[k], "tensor", peer)
+        for k, peer in enumerate(peers)
+    ]
+    whole[own, :] = piece[...]
+    for copy in copies:
+        copy.wait()
+
+
+def fold_kernel(partial, total, slots, sent, landed):
+    me, peers = meet("tensor")
+    rows = total.shape[0]
+    copies = []
+    for k, peer in enumerate(peers):
+        block = partial.at[pl.ds(pl.multiple_of(peer * rows, rows), rows)]
+        copies.append(push(block, slots.at[k], sent.at[k], landed.at[k], "tensor", peer))
+    own = pl.ds(pl.multiple_of(me * rows, rows), rows)
+    total[...] = partial[own, :].astype(jnp.float32)
+    for k, copy in enumerate(copies):
+        copy.wait()
+        total[...] += slots[k].astype(jnp.float32)
+
+
+def total_kernel(axis, piece, total, slots, sent, landed):
+    me, peers = meet(axis)
+    copies = [
+        push(piece, slots.at[me], sent.at[k], landed.at[k], axis, peer)
+        for k, peer in enumerate(peers)
+    ]
+    slots[pl.ds(me, 1)] = piece[...][None]
+    for copy in copies:
+        copy.wait()
+    result = slots[0]
+    for k in range(1, slots.shape[0]):
+        result = result + slots[k]
+    total[...] = result
+
+
+def exchange(kernel, item, out, slots, axis, number, name):
+    count = lax.axis_size(axis)
+    scratch = [] if slots is None else [pltpu.VMEM(slots, item.dtype)]
+    return pl.pallas_call(
+        kernel,
+        out_shape=jax.ShapeDtypeStruct(*out),
+        in_specs=[pl.BlockSpec(memory_space=pltpu.VMEM)],
+        out_specs=pl.BlockSpec(memory_space=pltpu.VMEM),
+        scratch_shapes=scratch
+        + [pltpu.SemaphoreType.DMA((count - 1,)), pltpu.SemaphoreType.DMA((count - 1,))],
+        compiler_params=pltpu.CompilerParams(
+            collective_id=number, has_side_effects=True, vmem_limit_bytes=24 * 2**20
+        ),
+        name=name,
+    )(item)
+
+
 def spread_rows(piece):
-    return lax.all_gather(piece, "tensor", axis=0, tiled=True)
+    rows, width = piece.shape
+    whole = (rows * lax.axis_size("tensor"), width)
+    return exchange(spread_kernel, piece, (whole, piece.dtype), None, "tensor", 1, "spread")
 
 
 def fold_rows(partial_sum):
-    return lax.psum_scatter(
-        partial_sum.astype(jnp.bfloat16), "tensor", scatter_dimension=0, tiled=True
-    ).astype(jnp.float32)
+    count = lax.axis_size("tensor")
+    rows, width = partial_sum.shape[0] // count, partial_sum.shape[1]
+    return exchange(
+        fold_kernel, partial_sum.astype(jnp.bfloat16), ((rows, width), jnp.float32),
+        (count - 1, rows, width), "tensor", 2, "fold",
+    )
+
+
+def total_over(item, axis, number):
+    return exchange(
+        functools.partial(total_kernel, axis), item, (item.shape, item.dtype),
+        (lax.axis_size(axis), *item.shape), axis, number, "total_" + axis,
+    )
 
 
 def swap_cores(block):
@@ -250,7 +349,7 @@
     return (layer_out, saved)
 
 
-def layer_backward(layer_grad, saved, clips, weights):
+def layer_backward(layer_grad, saved, clips, weights, prior):
     gains, shifts, qkv_w, bias_pair, output_w, expand_w, expand_b, reduce_w = weights
     (
         layer_in, normed, query, query_t, keys, values, mixed_t, logs, resid_mid, normed_mid,
@@ -265,7 +364,7 @@
     grad_reduce = inner_rows(activated, grad_all).astype(jnp.bfloat16)
     grad_expand_bias = jnp.sum(grad_expanded, axis=0, dtype=jnp.float32)
     grad_expand = inner_rows(normed_mid, grad_expanded).astype(jnp.bfloat16)
-    feed_sum = sum_half(grad_expand, grad_reduce)
+    feed_sum = sum_half(grad_expand, grad_reduce, prior)
     mid_back = jax.vjp(norm_rows, resid_mid, gains[1], shifts[1])[1]
     grad_mid_norm, grad_gain_mid, grad_shift_mid = mid_back(grad_normed_mid)
     grad_mid = grad_out + grad_mid_norm
@@ -281,8 +380,8 @@
     grad_qkv_w = inner_rows(normed, grad_qkv).astype(jnp.bfloat16)
     half = grad_qkv_w.shape[0] // 2
     half_out = grad_output.shape[0] // 2
-    qkv_sum = sum_half(grad_qkv_w[:half], grad_qkv_w[half:])
-    output_sum = sum_half(grad_output[:half_out], grad_output[half_out:])
+    qkv_sum = sum_half(grad_qkv_w[:half], grad_qkv_w[half:], feed_sum)
+    output_sum = sum_half(grad_output[:half_out], grad_output[half_out:], feed_sum)
     qkv_bias = jnp.sum(grad_qkv, axis=0, dtype=jnp.float32)
     in_back = jax.vjp(norm_rows, layer_in.astype(jnp.float32), gains[0], shifts[0])[1]
     grad_in_norm, grad_gain_in, grad_shift_in = in_back(grad_normed)
@@ -297,11 +396,14 @@
     return (input_grad, (feed_sum, qkv_sum, output_sum), norms, biases)
 
 
-def sum_half(first, second):
+def sum_half(first, second, prior):
     core = lax.axis_index("pipe") == 0
     kept = jnp.where(core, first, second)
     got = swap_cores(jnp.where(core, second, first))
-    return lax.psum(kept + got, "seq")
+    half = kept + got
+    if prior is not None:
+        half, _ = lax.optimization_barrier((half, prior))
+    return lax.psum(half, "seq")
 
 
 def shards(
@@ -341,7 +443,7 @@
     grads, sums, norms, biases = [None] * 2, [None] * 2, [None] * 2, [None] * 2
     for number in (1, 0):
         grad, sums[number], norms[number], biases[number] = layer_backward(
-            grad, saved[number], clips, weights[number]
+            grad, saved[number], clips, weights[number], None if number == 1 else sums[1][1]
         )
         grads[number] = grad
 
@@ -363,10 +465,22 @@
     grad_expand, grad_reduce = both_halves(0)
     grad_qkv = jnp.concatenate(both_halves(1), axis=0)
     grad_output = jnp.concatenate(both_halves(2), axis=0)
-    norm_sum = lax.psum(jnp.stack(norms), ("pipe", "seq", "tensor"))
-    norm_sum = lax.dynamic_index_in_dim(norm_sum, core, 0, keepdims=False)
-    bias_sum = lax.psum(jnp.stack(biases), ("pipe", "seq"))
-    bias_sum = lax.dynamic_index_in_dim(bias_sum, core, 0, keepdims=False)
+    norm_rows_all = jnp.pad(jnp.concatenate(norms), ((0, 4), (0, 0)))
+    norm_rows_all = total_over(norm_rows_all, "tensor", 3)
+    model = norm_rows_all.shape[1]
+    length = biases[0].shape[0]
+    bias_rows = [
+        jnp.pad(item, (0, -length % model)).reshape(-1, model) for item in biases
+    ]
+    packed = total_over(
+        jnp.concatenate([norm_rows_all[:6], bias_rows[0], norm_rows_all[6:12], bias_rows[1]]),
+        "seq", 4,
+    )
+    half_rows = packed.shape[0] // 2
+    first, second = packed[:half_rows], packed[half_rows:]
+    packed = jnp.where(low_core, first, second) + swap_cores(jnp.where(low_core, second, first))
+    norm_sum = packed[:6]
+    bias_sum = packed[6:].reshape(-1)[:length]
     width = proj_bias.shape[-1]
     return (
         states,

time: 855 us -> 681 us (0.80)
  Pallas kernels: 58.6 us -> 301 us
  waiting for transfers between devices: 373 us -> 186 us
  blocking collectives: 199 us -> 13.3 us
  other arithmetic: 61.4 us -> 38.7 us
  local copies, waits for them, and re-layouts: 66.5 us -> 54.9 us
    pallas_call x0 -> x18, Pallas kernels: none -> 230 us  [exchange(): pl.pallas_call(kernel, out_shape=jax.ShapeDtypeStruct(*out), in_specs=[pl...]
    reduce_scatter x8 -> x0, waiting for transfers between devices: 154 us -> none  [fold_rows(): lax.psum_scatter(partial_sum.astype(jnp.bfloat16), 'tensor', scatter_dime...]
    all_gather x8 -> x0, blocking collectives: 113 us -> none  [spread_rows(): return lax.all_gather(piece, 'tensor', axis=0, tiled=True)]
    psum x2 -> x0, blocking collectives: 72.2 us -> none  [the longest x1 43.2 us: shards(): norm_sum = lax.psum(jnp.stack(norms), ('pipe', 'seq', 'tensor'))]
    all_gather x2, waiting for transfers between devices: 67.7 us -> 51.8 us  [gather_window(): return lax.all_gather(block, 'seq', axis=0, tiled=True)]
    reduce_scatter x2, waiting for transfers between devices: 65.6 us -> 50.5 us  [return_window(): return lax.psum_scatter(terms, 'seq', scatter_dimension=0, tiled=True)]
    reduce_sum x8 -> x6, other arithmetic: 11.5 us -> 2.32 us  [norm_rows(): return center * lax.rsqrt(spread + EPS) * gain + shift]
    unnamed x184 -> x228, local copies, waits for them, and re-layouts: 31.9 us -> 24.8 us
  transfers between devices with their start and end apart: 32 -> 28, of which waited for: 14 -> 9; matrix products, arithmetic and copies ran while one was open for 10% -> 12% of each run, Pallas kernels for 2% -> 24%
where the time goes in v2:
time: 681 us; the launch traced here: 674 us
  Pallas kernels  301 us (44%)
  waiting for transfers between devices  186 us (27%)
  matrix products  55.3 us (8%)
  local copies, waits for them, and re-layouts  54.9 us (8%)
  other arithmetic  38.7 us (6%)
  between operations  16.5 us (2%)
  blocking collectives  13.3 us (2%)
  starting transfers between devices  8.68 us (1%)
    pallas_call x18, Pallas kernels, exchange(): pl.pallas_call(kernel, out_shape=jax.ShapeDtypeStruct(*out), in_specs=[pl...  230 us
    psum x4, waiting for transfers between devices, sum_half(): return lax.psum(half, 'seq')  81.8 us
    all_gather x2, waiting for transfers between devices, gather_window(): return lax.all_gather(block, 'seq', axis=0, tiled=True)  51.8 us
    reduce_scatter x2, waiting for transfers between devices, return_window(): return lax.psum_scatter(terms, 'seq', scatter_dimension=0, tiled=True)  50.5 us
    pallas_call x2, Pallas kernels, backward_attention(): pl.pallas_call(attend_back_kernel, out_shape=(jax.ShapeDtypeStruct((width...  38.4 us
    pallas_call x2, Pallas kernels, forward_attention(): pl.pallas_call(attend_kernel, out_shape=(jax.ShapeDtypeStruct((width, row...  32 us
    unnamed x228, local copies, waits for them, and re-layouts  24.8 us
    dot_general x8, matrix products, matmul(): return jnp.dot(left, right, preferred_element_type=jnp.float32)  21.9 us
  transfers between devices with their start and end apart: 28, of which 9 were waited for; matrix products, arithmetic and copies ran while one was open for 12% of the time, Pallas kernels for 24%

profile of v2, /device:TPU:0, one launch (start us, length us, event | category | flops | bytes accessed | tf_op | source)
XLA Modules:
  0.0 673.7 jit_solution(3029431260631367630)
XLA Ops:
  12.6 15.8 %spread.8 = bf16[640,768]{1,0:T(8,128)(2,1)S(1)} custom-call(bf16[160,768]{1,0:T(8,128)(2,1)S(1)} %fusion.30.piece), custom_call_target="tpu_custom_call" | custom-call | tf_op jit(solution)/shard_map/spread/pallas_call | solution.py:116
  32.4 13.3 %all-gather = s32[1,2560]{1,0:T(1,128)S(1)} all-gather(s32[1,640]{1,0:T(1,128)S(1)} %dynamic-slice_add_fusion.marks), channel_id=2, replica_groups=mesh['pipe'=2,'seq'=4,'tensor'=4] {'seq'}, dimensions={1}, use_global_device_ids=true | all-gather | bytes 12800 | tf_op jit(solution)/shard_map/all_gather | solution.py:168
  51.0 24.7 %all-gather.4.cloned.1.call-done = bf16[2560,384]{0,1:T(8,128)(2,1)} async-done(((bf16[640,384]{0,1:T(8,128)(2,1)}), bf16[2560,384]{0,1:T(8,128)(2,1)}) %all-gather.4.cloned.1.call-update) | async-done | bytes 1966096 | tf_op jit(solution)/shard_map/all_gather | solution.py:168
  82.0 16.1 %attend.2 = (bf16[192,640]{1,0:T(8,128)(2,1)S(1)}, f32[8,640]{1,0:T(8,128)S(1)}) custom-call(s32[2]{0:T(128)S(1)} %pad_add_fusion.span, bf16[2560,192]{1,0:T(8,128)(2,1)S(1)} %copy.35.keys, bf16[192,2560]{1,0:T(8,128)(2,1)S(1)} %copy-done.11, bf16[192,640]{1,0:T(8,128)(2,1)S(1)} %get-tuple-element.114.query_t, s32[2560,1]{1,0:T(8,128)S(1)} %copy.36.key_marks, ...), custom_call_target="tpu_custom_call" | custom-call | tf_op jit(solution)/shard_map/attend/pallas_call | solution.py:282
  99.6 14.1 %fold.8 = f32[160,768]{1,0:T(8,128)S(1)} custom-call(bf16[640,768]{1,0:T(8,128)(2,1)S(1)} %convolution_convert_fusion.5.partial), custom_call_target="tpu_custom_call" | custom-call | tf_op jit(solution)/shard_map/fold/pallas_call | solution.py:116
  114.3 14.2 %spread.9 = bf16[640,768]{1,0:T(8,128)(2,1)S(1)} custom-call(bf16[160,768]{1,0:T(8,128)(2,1)S(1)} %add_convert_fusion.9.piece), custom_call_target="tpu_custom_call" | custom-call | tf_op jit(solution)/shard_map/spread/pallas_call | solution.py:116
  136.9 13.3 %fold.9 = f32[160,768]{1,0:T(8,128)S(1)} custom-call(bf16[640,768]{1,0:T(8,128)(2,1)S(1)} %convolution_convert_fusion.11.partial), custom_call_target="tpu_custom_call" | custom-call | tf_op jit(solution)/shard_map/fold/pallas_call | solution.py:116
  151.2 15.1 %spread.10 = bf16[640,768]{1,0:T(8,128)(2,1)S(1)} custom-call(bf16[160,768]{1,0:T(8,128)(2,1)S(1)} %fusion.27.piece), custom_call_target="tpu_custom_call" | custom-call | tf_op jit(solution)/shard_map/spread/pallas_call | solution.py:116
  185.4 27.2 %all-gather.6.cloned.1.call-done = bf16[2560,384]{0,1:T(8,128)(2,1)} async-done(((bf16[640,384]{0,1:T(8,128)(2,1)}), bf16[2560,384]{0,1:T(8,128)(2,1)}) %all-gather.6.cloned.1.call-update) | async-done | bytes 1966096 | tf_op jit(solution)/shard_map/all_gather | solution.py:168
  223.4 15.8 %attend.3 = (bf16[192,640]{1,0:T(8,128)(2,1)S(1)}, f32[8,640]{1,0:T(8,128)S(1)}) custom-call(s32[2]{0:T(128)S(1)} %pad_add_fusion.span, bf16[2560,192]{1,0:T(8,128)(2,1)S(1)} %copy-done, bf16[192,2560]{1,0:T(8,128)(2,1)S(1)} %copy-done.10, bf16[192,640]{1,0:T(8,128)(2,1)S(1)} %get-tuple-element.116.query_t, s32[2560,1]{1,0:T(8,128)S(1)} %copy.36.key_marks, ...), custom_call_target="tpu_custom_call" | custom-call | tf_op jit(solution)/shard_map/attend/pallas_call | solution.py:282
  241.0 13.9 %fold.10 = f32[160,768]{1,0:T(8,128)S(1)} custom-call(bf16[640,768]{1,0:T(8,128)(2,1)S(1)} %convolution_convert_fusion.4.partial), custom_call_target="tpu_custom_call" | custom-call | tf_op jit(solution)/shard_map/fold/pallas_call | solution.py:116
  255.5 14.2 %spread.11 = bf16[640,768]{1,0:T(8,128)(2,1)S(1)} custom-call(bf16[160,768]{1,0:T(8,128)(2,1)S(1)} %add_convert_fusion.7.piece), custom_call_target="tpu_custom_call" | custom-call | tf_op jit(solution)/shard_map/spread/pallas_call | solution.py:116
  319.1 19.1 %attend_back.2 = (bf16[192,640]{1,0:T(8,128)(2,1)S(1)}, bf16[2560,192]{1,0:T(8,128)(2,1)S(1)}, bf16[2560,192]{1,0:T(8,128)(2,1)S(1)}) custom-call(s32[2]{0:T(128)S(1)} %pad_add_fusion.span, bf16[2560,192]{1,0:T(8,128)(2,1)S(1)} %copy-done.1, bf16[192,2560]{1,0:T(8,128)(2,1)S(1)} %copy-done.9, bf16[2560,192]{1,0:T(8,128)(2,1)S(1)} %copy-done.3, ...), custom_call_target="tpu_custom_call" | custom-call | tf_op jit(solution)/shard_map/attend_back/pallas_call | solution.py:299
  353.2 26.6 %reduce-scatter.3.cloned.1.call-done = bf16[640,384]{1,0:T(8,128)(2,1)} async-done(((bf16[2560,384]{1,0:T(8,128)(2,1)}), bf16[640,384]{1,0:T(8,128)(2,1)}) %reduce-scatter.3.cloned.1.call-update) | async-done | bytes 491536 | tf_op jit(solution)/shard_map/reduce_scatter | solution.py:176
  382.5 13.7 %fold.13 = f32[160,768]{1,0:T(8,128)S(1)} custom-call(bf16[640,768]{1,0:T(8,128)(2,1)S(1)} %convolution_convert_fusion.8.partial), custom_call_target="tpu_custom_call" | custom-call | tf_op jit(solution)/shard_map/fold/pallas_call | solution.py:116
  397.1 14.3 %spread.14 = bf16[640,768]{1,0:T(8,128)(2,1)S(1)} custom-call(bf16[160,768]{1,0:T(8,128)(2,1)S(1)} %get-tuple-element.109.piece), custom_call_target="tpu_custom_call" | custom-call | tf_op jit(solution)/shard_map/spread/pallas_call | solution.py:116
  419.9 13.6 %fold.14 = f32[160,768]{1,0:T(8,128)S(1)} custom-call(bf16[640,768]{1,0:T(8,128)(2,1)S(1)} %convolution_convert_fusion.7.partial), custom_call_target="tpu_custom_call" | custom-call | tf_op jit(solution)/shard_map/fold/pallas_call | solution.py:116
  440.7 36.8 %all-reduce.11.cloned.1.call-done = bf16[384,576]{0,1:T(8,128)(2,1)} async-done(((bf16[384,576]{0,1:T(8,128)(2,1)}), bf16[384,576]{0,1:T(8,128)(2,1)}) %all-reduce.11.cloned.1.call-update) | async-done | bytes 442384 | tf_op jit(solution)/shard_map/psum | solution.py:406
  479.9 13.0 %spread.15 = bf16[640,768]{1,0:T(8,128)(2,1)S(1)} custom-call(bf16[160,768]{1,0:T(8,128)(2,1)S(1)} %get-tuple-element.110.piece), custom_call_target="tpu_custom_call" | custom-call | tf_op jit(solution)/shard_map/spread/pallas_call | solution.py:116
  503.3 19.3 %attend_back.3 = (bf16[192,640]{1,0:T(8,128)(2,1)S(1)}, bf16[2560,192]{1,0:T(8,128)(2,1)S(1)}, bf16[2560,192]{1,0:T(8,128)(2,1)S(1)}) custom-call(s32[2]{0:T(128)S(1)} %pad_add_fusion.span, bf16[2560,192]{1,0:T(8,128)(2,1)S(1)} %copy.35.keys, bf16[192,2560]{1,0:T(8,128)(2,1)S(1)} %copy-done.4, bf16[2560,192]{1,0:T(8,128)(2,1)S(1)} %copy-done.2, ...), custom_call_target="tpu_custom_call" | custom-call | tf_op jit(solution)/shard_map/attend_back/pallas_call | solution.py:299
  530.1 14.1 %fold.11 = f32[160,768]{1,0:T(8,128)S(1)} custom-call(bf16[640,768]{1,0:T(8,128)(2,1)S(1)} %convolution_convert_fusion.10.partial), custom_call_target="tpu_custom_call" | custom-call | tf_op jit(solution)/shard_map/fold/pallas_call | solution.py:116
  555.9 23.9 %reduce-scatter.5.cloned.1.call-done = bf16[640,384]{1,0:T(8,128)(2,1)} async-done(((bf16[2560,384]{1,0:T(8,128)(2,1)}), bf16[640,384]{1,0:T(8,128)(2,1)}) %reduce-scatter.5.cloned.1.call-update) | async-done | bytes 491536 | tf_op jit(solution)/shard_map/reduce_scatter | solution.py:176
  582.0 14.2 %fold.15 = f32[160,768]{1,0:T(8,128)S(1)} custom-call(bf16[640,768]{1,0:T(8,128)(2,1)S(1)} %convolution_convert_fusion.6.partial), custom_call_target="tpu_custom_call" | custom-call | tf_op jit(solution)/shard_map/fold/pallas_call | solution.py:116
  617.8 41.8 %all-reduce.15.cloned.1.call-done = (bf16[384,576]{0,1:T(8,128)(2,1)}, bf16[96,768]{1,0:T(8,128)(2,1)}, bf16[96,768]{1,0:T(8,128)(2,1)}) async-done(((bf16[384,576]{0,1:T(8,128)(2,1)}, bf16[96,768]{1,0:T(8,128)(2,1)}, bf16[96,768]{1,0:T(8,128)(2,1)}), (bf16[384,576]{0,1:T(8,128)(2,1)}, bf16[96,768]{1,0:T(8,128)(2,1)}, bf16[96,768]{1,0:T(8,128)(2,1)})) %all-reduce.15.cloned.1.call-update) | async-done | bytes 737296 | tf_op jit(solution)/shard_map/psum | solution.py:406
  (449 shorter events, 209.3 us)
Async XLA Ops:
  7.2 68.4 %all-gather.4.cloned.1.call-start = ((), (), s32[]{:S(2)}) async-start(), calls=%async_computation.2 | async-start | bytes 2457600 | tf_op jit(solution)/shard_map/all_gather | solution.py:168
  7.3 3.9 collective-permute-start.3
  7.8 3.5 collective-permute-start
  7.9 3.5 collective-permute-start.1
  10.7 17.7 %collective-permute-start.2 = (bf16[768,576]{0,1:T(8,128)(2,1)S(1)}, bf16[768,576]{0,1:T(8,128)(2,1)}, u32[]{:S(2)}, u32[]{:S(2)}) collective-permute-start(bf16[768,576]{0,1:T(8,128)(2,1)S(1)} %pad_maximum_fusion.2), channel_id=1, source_target_pairs={{0,16},{16,0},{1,17},{17,1},{2,18},{18,2},{3,19},{19,3},{4,20},{20... | collective-permute-start | bytes 2654216 | tf_op jit(solution)/shard_map/ppermute | solution.py:153
  30.2 182.3 %all-gather.6.cloned.1.call-start = ((), (), s32[]{:S(2)}) async-start(), calls=%async_computation.3 | async-start | bytes 2457600 | tf_op jit(solution)/shard_map/all_gather | solution.py:168
  30.3 19.9 %collective-permute-start.6 = (f32[768]{0:T(1024)S(1)}, f32[768]{0:T(1024)S(1)}, u32[]{:S(2)}, u32[]{:S(2)}) collective-permute-start(f32[768]{0:T(1024)S(1)} %reduce.7), channel_id=1, source_target_pairs={{0,16},{16,0},{1,17},{17,1},{2,18},{18,2},{3,19},{19,3},{4,20},{20... | collective-permute-start | bytes 9224 | tf_op jit(solution)/shard_map/ppermute | solution.py:153
  31.8 66.3 %collective-permute-start.4 = (bf16[192,768]{1,0:T(8,128)(2,1)}, bf16[192,768]{1,0:T(8,128)(2,1)}, u32[]{:S(2)}, u32[]{:S(2)}) collective-permute-start(bf16[192,768]{1,0:T(8,128)(2,1)} %bitcast.16), channel_id=1, source_target_pairs={{0,16},{16,0},{1,17},{17,1},{2,18},{18,2},{3,19},{19,3},{4,20},{20... | collective-permute-start | bytes 884744 | tf_op jit(solution)/shard_map/ppermute | solution.py:153
  31.9 103.1 %collective-permute-start.7 = (bf16[768,768]{1,0:T(8,128)(2,1)}, bf16[768,768]{1,0:T(8,128)(2,1)}, u32[]{:S(2)}, u32[]{:S(2)}) collective-permute-start(bf16[768,768]{1,0:T(8,128)(2,1)} %bitcast.235), channel_id=1, source_target_pairs={{0,16},{16,0},{1,17},{17,1},{2,18},{18,2},{3,19},{19,3},{4,20},{20... | collective-permute-start | bytes 3538952 | tf_op jit(solution)/shard_map/ppermute | solution.py:153
  32.3 96.3 %collective-permute-start.5 = (bf16[768,768]{1,0:T(8,128)(2,1)}, bf16[768,768]{1,0:T(8,128)(2,1)}, u32[]{:S(2)}, u32[]{:S(2)}) collective-permute-start(bf16[768,768]{1,0:T(8,128)(2,1)} %bitcast.234), channel_id=1, source_target_pairs={{0,16},{16,0},{1,17},{17,1},{2,18},{18,2},{3,19},{19,3},{4,20},{20... | collective-permute-start | bytes 3538952 | tf_op jit(solution)/shard_map/ppermute | solution.py:153
  170.5 209.2 %reduce-scatter.3.cloned.1.call-start = ((), (), s32[]{:S(2)}) async-start(), calls=%async_computation.4 | async-start | bytes 2457600 | tf_op jit(solution)/shard_map/reduce_scatter | solution.py:176
  341.0 96.8 %all-reduce.9.cloned.1.call-start = ((), (), s32[]{:S(2)}) async-start(), calls=%async_computation.6 | async-start | bytes 2359296 | tf_op jit(solution)/shard_map/psum | solution.py:406
  346.6 3.5 collective-permute-start.14
  353.1 124.4 %all-reduce.11.cloned.1.call-start = ((), (), s32[]{:S(2)}) async-start(), calls=%async_computation.7 | async-start | bytes 884736 | tf_op jit(solution)/shard_map/psum | solution.py:406
  416.8 21.0 %collective-permute-start.12 = (bf16[768,768]{1,0:T(8,128)(2,1)}, bf16[768,768]{1,0:T(8,128)(2,1)}, u32[]{:S(2)}, u32[]{:S(2)}) collective-permute-start(bf16[768,768]{1,0:T(8,128)(2,1)} %get-tuple-element.153), channel_id=1, source_target_pairs={{0,16},{16,0},{1,17},{17,1},{2,18},{18,2},{3,19},{19,3},{4,20},{20... | collective-permute-start | bytes 3538952 | tf_op jit(solution)/shard_map/ppermute | solution.py:153
  418.7 15.0 %collective-permute-start.13 = (bf16[384,576]{0,1:T(8,128)(2,1)S(1)}, bf16[384,576]{0,1:T(8,128)(2,1)S(1)}, u32[]{:S(2)}, u32[]{:S(2)}) collective-permute-start(bf16[384,576]{0,1:T(8,128)(2,1)S(1)} %broadcast_select_fusion.26), channel_id=1, source_target_pairs={{0,16},{16,0},{1,17},{17,1},{2,18},{18,2},{3,19},{19,3},{4,20},{20... | collective-permute-start | bytes 1327112 | tf_op jit(solution)/shard_map/ppermute | solution.py:153
  437.8 107.4 %all-reduce.13.cloned.1.call-start = ((), (), s32[]{:S(2)}) async-start(), calls=%async_computation.8 | async-start | bytes 2359296 | tf_op jit(solution)/shard_map/psum | solution.py:406
  477.5 102.3 %reduce-scatter.5.cloned.1.call-start = ((), (), s32[]{:S(2)}) async-start(), calls=%async_computation.5 | async-start | bytes 2457600 | tf_op jit(solution)/shard_map/reduce_scatter | solution.py:176
  525.3 134.4 %all-reduce.15.cloned.1.call-start = ((), (), s32[]{:S(2)}) async-start(), calls=%async_computation.9 | async-start | bytes 1474560 | tf_op jit(solution)/shard_map/psum | solution.py:406
  527.0 17.5 %collective-permute-start.17 = (bf16[96,768]{1,0:T(8,128)(2,1)S(1)}, bf16[96,768]{1,0:T(8,128)(2,1)S(1)}, u32[]{:S(2)}, u32[]{:S(2)}) collective-permute-start(bf16[96,768]{1,0:T(8,128)(2,1)S(1)} %broadcast_select_fusion.42), channel_id=1, source_target_pairs={{0,16},{16,0},{1,17},{17,1},{2,18},{18,2},{3,19},{19,3},{4,20},{20... | collective-permute-start | bytes 442376 | tf_op jit(solution)/shard_map/ppermute | solution.py:153
  544.4 3.7 collective-permute-start.8
  547.6 4.1 collective-permute-start.19
  610.4 7.4 %collective-permute-start.9 = (bf16[160,768]{1,0:T(8,128)(2,1)}, bf16[160,768]{1,0:T(8,128)(2,1)S(1)}, u32[]{:S(2)}, u32[]{:S(2)}) collective-permute-start(bf16[160,768]{1,0:T(8,128)(2,1)} %get-tuple-element.76), channel_id=1, source_target_pairs={{0,16},{16,0},{1,17},{17,1},{2,18},{18,2},{3,19},{19,3},{4,20},{20... | collective-permute-start | bytes 737288 | tf_op jit(solution)/shard_map/ppermute | solution.py:153
  660.8 3.3 collective-permute-start.15
  (118 other events, 1322.1 us)
Sparse Core Ops, SparseCore 0:
  30.3 45.2 all-gather.3
  170.7 41.8 all-gather.5
  341.1 38.6 reduce-scatter.2
  382.6 55.1 all-reduce.8
  440.5 36.9 all-reduce.10
  480.4 55.7 all-reduce.12
  538.7 41.0 reduce-scatter.4
  616.0 43.5 all-reduce.14

commit v3 on v2

--- a/solution.py
+++ b/solution.py
@@ -93,6 +93,17 @@
     for k, copy in enumerate(copies):
         copy.wait()
         total[...] += slots[k].astype(jnp.float32)
+
+
+def marks_kernel(piece, whole, sent, landed):
+    me, peers = meet("seq")
+    copies = [
+        push(piece, whole.at[me], sent.at[k], landed.at[k], "seq", peer)
+        for k, peer in enumerate(peers)
+    ]
+    whole[pl.ds(me, 1)] = piece[...][None]
+    for copy in copies:
+        copy.wait()
 
 
 def total_kernel(axis, piece, total, slots, sent, landed):
@@ -313,7 +324,14 @@
 
 def clip_window(clip_here):
     marks = clip_here + 1
-    key_marks = gather_window(marks)
+    if whole_row():
+        count = lax.axis_size("seq")
+        key_marks = exchange(
+            marks_kernel, marks.reshape(-1, KEY_TILE),
+            ((count, marks.shape[0] // KEY_TILE, KEY_TILE), marks.dtype), None, "seq", 5, "marks",
+        ).reshape(-1)
+    else:
+        key_marks = gather_window(marks)
     tiles = key_marks.reshape(-1, KEY_TILE)
     hit = jnp.any((tiles >= marks[0]) & (tiles <= marks[-1]), axis=1)
     place = jnp.arange(tiles.shape[0], dtype=jnp.int32)
@@ -364,7 +382,11 @@
     grad_reduce = inner_rows(activated, grad_all).astype(jnp.bfloat16)
     grad_expand_bias = jnp.sum(grad_expanded, axis=0, dtype=jnp.float32)
     grad_expand = inner_rows(normed_mid, grad_expanded).astype(jnp.bfloat16)
-    feed_sum = sum_half(grad_expand, grad_reduce, prior)
+    feed_half = add_cores(grad_expand, grad_reduce)
+    if prior is None:
+        early = (lax.psum(feed_half, "seq"),)
+    else:
+        early = sum_after((prior[1], prior[2], feed_half), prior[0])
     mid_back = jax.vjp(norm_rows, resid_mid, gains[1], shifts[1])[1]
     grad_mid_norm, grad_gain_mid, grad_shift_mid = mid_back(grad_normed_mid)
     grad_mid = grad_out + grad_mid_norm
@@ -374,14 +396,15 @@
         keys, keys.T, values, query, query_t, grad_mixed, grad_mixed.T, mixed_t, logs, clips
     )
     grad_output = matmul(mixed_t, grad_branch).astype(jnp.bfloat16)
-    grad_keyval = return_window(jnp.concatenate([key_terms, value_terms], axis=1))
+    terms = jnp.concatenate([key_terms, value_terms], axis=1)
+    grad_keyval = return_window(terms)
     grad_qkv = jnp.concatenate([query_grad_t.T, grad_keyval], axis=1)
     grad_normed = fold_rows(times_trans(grad_qkv, qkv_w))
     grad_qkv_w = inner_rows(normed, grad_qkv).astype(jnp.bfloat16)
     half = grad_qkv_w.shape[0] // 2
     half_out = grad_output.shape[0] // 2
-    qkv_sum = sum_half(grad_qkv_w[:half], grad_qkv_w[half:], feed_sum)
-    output_sum = sum_half(grad_output[:half_out], grad_output[half_out:], feed_sum)
+    qkv_half = add_cores(grad_qkv_w[:half], grad_qkv_w[half:])
+    output_half = add_cores(grad_output[:half_out], grad_output[half_out:])
     qkv_bias = jnp.sum(grad_qkv, axis=0, dtype=jnp.float32)
     in_back = jax.vjp(norm_rows, layer_in.astype(jnp.float32), gains[0], shifts[0])[1]
     grad_in_norm, grad_gain_in, grad_shift_in = in_back(grad_normed)
@@ -393,17 +416,18 @@
         ]
     )
     biases = jnp.concatenate([qkv_bias, grad_expand_bias])
-    return (input_grad, (feed_sum, qkv_sum, output_sum), norms, biases)
-
-
-def sum_half(first, second, prior):
+    return (input_grad, (*early, qkv_half, output_half), norms, biases)
+
+
+def add_cores(first, second):
     core = lax.axis_index("pipe") == 0
     kept = jnp.where(core, first, second)
-    got = swap_cores(jnp.where(core, second, first))
-    half = kept + got
-    if prior is not None:
-        half, _ = lax.optimization_barrier((half, prior))
-    return lax.psum(half, "seq")
+    return kept + swap_cores(jnp.where(core, second, first))
+
+
+def sum_after(items, prior):
+    items, _ = lax.optimization_barrier((items, prior))
+    return lax.psum(items, "seq")
 
 
 def shards(
@@ -443,9 +467,15 @@
     grads, sums, norms, biases = [None] * 2, [None] * 2, [None] * 2, [None] * 2
     for number in (1, 0):
         grad, sums[number], norms[number], biases[number] = layer_backward(
-            grad, saved[number], clips, weights[number], None if number == 1 else sums[1][1]
+            grad, saved[number], clips, weights[number], None if number == 1 else sums[1]
         )
         grads[number] = grad
+
+    qkv_high, output_high, feed_low, qkv_half, output_half = sums[0]
+    sums = [
+        (feed_low, *sum_after((qkv_half, output_half), feed_low)),
+        (sums[1][0], qkv_high, output_high),
+    ]
 
     def both_batches(pair):
         mine = jnp.where(low_core, pair[0], pair[1])

time: 681 us -> 655 us (0.962)
  Pallas kernels: 301 us -> 253 us
  starting transfers between devices: 8.68 us -> 30.7 us
  blocking collectives: 13.3 us -> 0 us
    all_gather x2, waiting for transfers between devices: 51.8 us -> 80.1 us  [gather_window(): return lax.all_gather(block, 'seq', axis=0, tiled=True)]
    psum x4 -> x3, waiting for transfers between devices: 81.8 us -> 55.5 us  [the longest x2 54.5 us: sum_after(): return lax.psum(items, 'seq')]
    pallas_call x2, Pallas kernels: 38.4 us -> 19.1 us  [backward_attention(): pl.pallas_call(attend_back_kernel, out_shape=(jax.ShapeDtypeStruct((width...]
    pallas_call x2, Pallas kernels: 32 us -> 15.7 us  [forward_attention(): pl.pallas_call(attend_kernel, out_shape=(jax.ShapeDtypeStruct((width, row...]
    ppermute x20, starting transfers between devices: 7.72 us -> 21.3 us  [swap_cores(): return lax.ppermute(block, 'pipe', [(0, 1), (1, 0)])]
    all_gather x1 -> x0, blocking collectives: 13.3 us -> none  [gather_window(): return lax.all_gather(block, 'seq', axis=0, tiled=True)]
    pallas_call x18 -> x19, Pallas kernels: 230 us -> 218 us  [exchange(): pl.pallas_call(kernel, out_shape=jax.ShapeDtypeStruct(*out), in_specs=[pl...]
    psum x4 -> x3, starting transfers between devices: 0.38 us -> 9.03 us  [the longest x2 8.99 us: sum_after(): return lax.psum(items, 'seq')]
  transfers between devices with their start and end apart: 28 -> 27, of which waited for: 9 -> 6; matrix products, arithmetic and copies ran while one was open for 12% -> 13% of each run, Pallas kernels for 24% -> 25%
where the time goes in v3:
time: 655 us; the launch traced here: 646 us
  Pallas kernels  253 us (39%)
  waiting for transfers between devices  192 us (29%)
  local copies, waits for them, and re-layouts  56.2 us (9%)
  matrix products  54.5 us (8%)
  other arithmetic  43.6 us (7%)
  starting transfers between devices  30.7 us (5%)
  between operations  16.2 us (2%)
    pallas_call x19, Pallas kernels, exchange(): pl.pallas_call(kernel, out_shape=jax.ShapeDtypeStruct(*out), in_specs=[pl...  218 us
    all_gather x2, waiting for transfers between devices, gather_window(): return lax.all_gather(block, 'seq', axis=0, tiled=True)  80.1 us
    reduce_scatter x2, waiting for transfers between devices, return_window(): return lax.psum_scatter(terms, 'seq', scatter_dimension=0, tiled=True)  56.2 us
    psum x2, waiting for transfers between devices, sum_after(): return lax.psum(items, 'seq')  54.5 us
    unnamed x236, local copies, waits for them, and re-layouts  24.7 us
    dot_general x8, matrix products, matmul(): return jnp.dot(left, right, preferred_element_type=jnp.float32)  22 us
    ppermute x20, starting transfers between devices, swap_cores(): return lax.ppermute(block, 'pipe', [(0, 1), (1, 0)])  21.3 us
    pallas_call x2, Pallas kernels, backward_attention(): pl.pallas_call(attend_back_kernel, out_shape=(jax.ShapeDtypeStruct((width...  19.1 us
  transfers between devices with their start and end apart: 27, of which 6 were waited for; matrix products, arithmetic and copies ran while one was open for 13% of the time, Pallas kernels for 25%

profile of v3, /device:TPU:0, one launch (start us, length us, event | category | flops | bytes accessed | tf_op | source)
XLA Modules:
  0.0 645.6 jit_solution(16046452428943118651)
XLA Ops:
  12.6 15.8 %spread.8 = bf16[640,768]{1,0:T(8,128)(2,1)S(1)} custom-call(bf16[160,768]{1,0:T(8,128)(2,1)S(1)} %fusion.30.piece), custom_call_target="tpu_custom_call" | custom-call | tf_op jit(solution)/shard_map/spread/pallas_call | solution.py:127
  44.3 31.4 %all-gather.3.cloned.1.call-done = bf16[2560,384]{0,1:T(8,128)(2,1)} async-done(((bf16[640,384]{0,1:T(8,128)(2,1)}), bf16[2560,384]{0,1:T(8,128)(2,1)}) %all-gather.3.cloned.1.call-update) | async-done | bytes 1966096 | tf_op jit(solution)/shard_map/all_gather | solution.py:179
  91.4 9.9 %fold.8 = f32[160,768]{1,0:T(8,128)S(1)} custom-call(bf16[640,768]{1,0:T(8,128)(2,1)S(1)} %convolution_convert_fusion.5.partial), custom_call_target="tpu_custom_call" | custom-call | tf_op jit(solution)/shard_map/fold/pallas_call | solution.py:127
  102.0 10.8 %spread.9 = bf16[640,768]{1,0:T(8,128)(2,1)S(1)} custom-call(bf16[160,768]{1,0:T(8,128)(2,1)S(1)} %add_convert_fusion.9.piece), custom_call_target="tpu_custom_call" | custom-call | tf_op jit(solution)/shard_map/spread/pallas_call | solution.py:127
  121.1 9.8 %fold.9 = f32[160,768]{1,0:T(8,128)S(1)} custom-call(bf16[640,768]{1,0:T(8,128)(2,1)S(1)} %convolution_convert_fusion.11.partial), custom_call_target="tpu_custom_call" | custom-call | tf_op jit(solution)/shard_map/fold/pallas_call | solution.py:127
  132.0 12.9 %spread.10 = bf16[640,768]{1,0:T(8,128)(2,1)S(1)} custom-call(bf16[160,768]{1,0:T(8,128)(2,1)S(1)} %fusion.27.piece), custom_call_target="tpu_custom_call" | custom-call | tf_op jit(solution)/shard_map/spread/pallas_call | solution.py:127
  149.5 10.7 %spread.12 = bf16[640,768]{1,0:T(8,128)(2,1)S(1)} custom-call(bf16[160,768]{1,0:T(8,128)(2,1)S(1)} %dynamic-slice_bitcast_fusion.piece), custom_call_target="tpu_custom_call" | custom-call | tf_op jit(solution)/shard_map/spread/pallas_call | solution.py:127
  162.4 48.7 %all-gather.5.cloned.1.call-done = bf16[2560,384]{0,1:T(8,128)(2,1)} async-done(((bf16[640,384]{0,1:T(8,128)(2,1)}), bf16[2560,384]{0,1:T(8,128)(2,1)}) %all-gather.5.cloned.1.call-update) | async-done | bytes 1966096 | tf_op jit(solution)/shard_map/all_gather | solution.py:179
  229.0 9.9 %fold.10 = f32[160,768]{1,0:T(8,128)S(1)} custom-call(bf16[640,768]{1,0:T(8,128)(2,1)S(1)} %convolution_convert_fusion.4.partial), custom_call_target="tpu_custom_call" | custom-call | tf_op jit(solution)/shard_map/fold/pallas_call | solution.py:127
  239.5 10.5 %spread.11 = bf16[640,768]{1,0:T(8,128)(2,1)S(1)} custom-call(bf16[160,768]{1,0:T(8,128)(2,1)S(1)} %add_convert_fusion.7.piece), custom_call_target="tpu_custom_call" | custom-call | tf_op jit(solution)/shard_map/spread/pallas_call | solution.py:127
  263.8 14.9 %fold.12 = f32[160,768]{1,0:T(8,128)S(1)} custom-call(bf16[640,768]{1,0:T(8,128)(2,1)S(1)} %convolution_convert_fusion.9.partial), custom_call_target="tpu_custom_call" | custom-call | tf_op jit(solution)/shard_map/fold/pallas_call | solution.py:127
  280.8 14.4 %spread.13 = bf16[640,768]{1,0:T(8,128)(2,1)S(1)} custom-call(bf16[160,768]{1,0:T(8,128)(2,1)S(1)} %fusion.66.piece), custom_call_target="tpu_custom_call" | custom-call | tf_op jit(solution)/shard_map/spread/pallas_call | solution.py:127
  308.3 9.5 %attend_back.2 = (bf16[192,640]{1,0:T(8,128)(2,1)S(1)}, bf16[2560,192]{1,0:T(8,128)(2,1)S(1)}, bf16[2560,192]{1,0:T(8,128)(2,1)S(1)}) custom-call(s32[2]{0:T(128)S(1)} %pad_add_fusion.span, bf16[2560,192]{1,0:T(8,128)(2,1)S(1)} %copy-done.1, bf16[192,2560]{1,0:T(8,128)(2,1)S(1)} %copy-done.7, bf16[2560,192]{1,0:T(8,128)(2,1)S(1)} %copy-done.3, ...), custom_call_target="tpu_custom_call" | custom-call | tf_op jit(solution)/shard_map/attend_back/pallas_call | solution.py:310
  343.4 8.7 %all-reduce.10.cloned.1.call-start = ((), (), s32[]{:S(2)}) async-start(), calls=%async_computation.7 | async-start | bytes 2359296 | tf_op jit(solution)/shard_map/psum | solution.py:430
  352.2 26.7 %reduce-scatter.3.cloned.1.call-done = bf16[640,384]{1,0:T(8,128)(2,1)} async-done(((bf16[2560,384]{1,0:T(8,128)(2,1)}), bf16[640,384]{1,0:T(8,128)(2,1)}) %reduce-scatter.3.cloned.1.call-update) | async-done | bytes 491536 | tf_op jit(solution)/shard_map/reduce_scatter | solution.py:187
  381.5 13.7 %fold.13 = f32[160,768]{1,0:T(8,128)S(1)} custom-call(bf16[640,768]{1,0:T(8,128)(2,1)S(1)} %convolution_convert_fusion.8.partial), custom_call_target="tpu_custom_call" | custom-call | tf_op jit(solution)/shard_map/fold/pallas_call | solution.py:127
  397.7 14.2 %spread.14 = bf16[640,768]{1,0:T(8,128)(2,1)S(1)} custom-call(bf16[160,768]{1,0:T(8,128)(2,1)S(1)} %get-tuple-element.112.piece), custom_call_target="tpu_custom_call" | custom-call | tf_op jit(solution)/shard_map/spread/pallas_call | solution.py:127
  419.8 13.7 %fold.14 = f32[160,768]{1,0:T(8,128)S(1)} custom-call(bf16[640,768]{1,0:T(8,128)(2,1)S(1)} %convolution_convert_fusion.7.partial), custom_call_target="tpu_custom_call" | custom-call | tf_op jit(solution)/shard_map/fold/pallas_call | solution.py:127
  439.0 14.2 %spread.15 = bf16[640,768]{1,0:T(8,128)(2,1)S(1)} custom-call(bf16[160,768]{1,0:T(8,128)(2,1)S(1)} %get-tuple-element.113.piece), custom_call_target="tpu_custom_call" | custom-call | tf_op jit(solution)/shard_map/spread/pallas_call | solution.py:127
  463.5 9.6 %attend_back.3 = (bf16[192,640]{1,0:T(8,128)(2,1)S(1)}, bf16[2560,192]{1,0:T(8,128)(2,1)S(1)}, bf16[2560,192]{1,0:T(8,128)(2,1)S(1)}) custom-call(s32[2]{0:T(128)S(1)} %pad_add_fusion.span, bf16[2560,192]{1,0:T(8,128)(2,1)S(1)} %copy.51.keys, bf16[192,2560]{1,0:T(8,128)(2,1)S(1)} %copy-done.4, bf16[2560,192]{1,0:T(8,128)(2,1)S(1)} %copy-done.2, ...), custom_call_target="tpu_custom_call" | custom-call | tf_op jit(solution)/shard_map/attend_back/pallas_call | solution.py:310
  479.5 9.9 %fold.11 = f32[160,768]{1,0:T(8,128)S(1)} custom-call(bf16[640,768]{1,0:T(8,128)(2,1)S(1)} %convolution_convert_fusion.10.partial), custom_call_target="tpu_custom_call" | custom-call | tf_op jit(solution)/shard_map/fold/pallas_call | solution.py:127
  508.8 29.5 %reduce-scatter.5.cloned.1.call-done = bf16[640,384]{1,0:T(8,128)(2,1)} async-done(((bf16[2560,384]{1,0:T(8,128)(2,1)}), bf16[640,384]{1,0:T(8,128)(2,1)}) %reduce-scatter.5.cloned.1.call-update) | async-done | bytes 491536 | tf_op jit(solution)/shard_map/reduce_scatter | solution.py:187
  544.4 14.7 %fold.15 = f32[160,768]{1,0:T(8,128)S(1)} custom-call(bf16[640,768]{1,0:T(8,128)(2,1)S(1)} %convolution_convert_fusion.6.partial), custom_call_target="tpu_custom_call" | custom-call | tf_op jit(solution)/shard_map/fold/pallas_call | solution.py:127
  577.2 54.5 %all-reduce.12.cloned.1.call-done = (bf16[384,576]{0,1:T(8,128)(2,1)}, bf16[384,576]{0,1:T(8,128)(2,1)}, bf16[96,768]{1,0:T(8,128)(2,1)}, bf16[96,768]{1,0:T(8,128)(2,1)}) async-done(((bf16[384,576]{0,1:T(8,128)(2,1)}, bf16[384,576]{0,1:T(8,128)(2,1)}, bf16[96,768]{1,0:T(8,128)(2,1)}, bf16[96,768]{1,0:T(8,128)(2,1)}), (bf16[384,576]{0,1:T(8,128)(2,1)}, bf16[384,576]{0,1:T(8,128)(2,1)}, ...) | async-done | bytes 1179664 | tf_op jit(solution)/shard_map/psum | solution.py:430
  (453 shorter events, 210.8 us)
Async XLA Ops:
  7.2 68.4 %all-gather.3.cloned.1.call-start = ((), (), s32[]{:S(2)}) async-start(), calls=%async_computation.2 | async-start | bytes 2457600 | tf_op jit(solution)/shard_map/all_gather | solution.py:179
  7.3 3.9 collective-permute-start.3
  7.8 3.6 collective-permute-start.1
  7.9 3.5 collective-permute-start
  10.7 17.7 %collective-permute-start.2 = (bf16[768,576]{0,1:T(8,128)(2,1)S(1)}, bf16[768,576]{0,1:T(8,128)(2,1)}, u32[]{:S(2)}, u32[]{:S(2)}) collective-permute-start(bf16[768,576]{0,1:T(8,128)(2,1)S(1)} %pad_maximum_fusion.2), channel_id=1, source_target_pairs={{0,16},{16,0},{1,17},{17,1},{2,18},{18,2},{3,19},{19,3},{4,20},{20... | collective-permute-start | bytes 2654216 | tf_op jit(solution)/shard_map/ppermute | solution.py:164
  30.2 180.9 %all-gather.5.cloned.1.call-start = ((), (), s32[]{:S(2)}) async-start(), calls=%async_computation.3 | async-start | bytes 2457600 | tf_op jit(solution)/shard_map/all_gather | solution.py:179
  30.2 59.7 %collective-permute-start.4 = (bf16[192,768]{1,0:T(8,128)(2,1)}, bf16[192,768]{1,0:T(8,128)(2,1)}, u32[]{:S(2)}, u32[]{:S(2)}) collective-permute-start(bf16[192,768]{1,0:T(8,128)(2,1)} %bitcast.15), channel_id=1, source_target_pairs={{0,16},{16,0},{1,17},{17,1},{2,18},{18,2},{3,19},{19,3},{4,20},{20... | collective-permute-start | bytes 884744 | tf_op jit(solution)/shard_map/ppermute | solution.py:164
  31.8 11.7 %collective-permute-start.6 = (f32[768]{0:T(1024)S(1)}, f32[768]{0:T(1024)S(1)}, u32[]{:S(2)}, u32[]{:S(2)}) collective-permute-start(f32[768]{0:T(1024)S(1)} %reduce.10), channel_id=1, source_target_pairs={{0,16},{16,0},{1,17},{17,1},{2,18},{18,2},{3,19},{19,3},{4,20},{20... | collective-permute-start | bytes 9224 | tf_op jit(solution)/shard_map/ppermute | solution.py:164
  31.9 81.0 %collective-permute-start.5 = (bf16[768,768]{1,0:T(8,128)(2,1)}, bf16[768,768]{1,0:T(8,128)(2,1)}, u32[]{:S(2)}, u32[]{:S(2)}) collective-permute-start(bf16[768,768]{1,0:T(8,128)(2,1)} %bitcast.232), channel_id=1, source_target_pairs={{0,16},{16,0},{1,17},{17,1},{2,18},{18,2},{3,19},{19,3},{4,20},{20... | collective-permute-start | bytes 3538952 | tf_op jit(solution)/shard_map/ppermute | solution.py:164
  32.3 86.9 %collective-permute-start.7 = (bf16[768,768]{1,0:T(8,128)(2,1)}, bf16[768,768]{1,0:T(8,128)(2,1)}, u32[]{:S(2)}, u32[]{:S(2)}) collective-permute-start(bf16[768,768]{1,0:T(8,128)(2,1)} %bitcast.233), channel_id=1, source_target_pairs={{0,16},{16,0},{1,17},{17,1},{2,18},{18,2},{3,19},{19,3},{4,20},{20... | collective-permute-start | bytes 3538952 | tf_op jit(solution)/shard_map/ppermute | solution.py:164
  149.2 229.6 %reduce-scatter.3.cloned.1.call-start = ((), (), s32[]{:S(2)}) async-start(), calls=%async_computation.4 | async-start | bytes 2457600 | tf_op jit(solution)/shard_map/reduce_scatter | solution.py:187
  320.6 116.2 %all-reduce.8.cloned.1.call-start = ((), (), s32[]{:S(2)}) async-start(), calls=%async_computation.6 | async-start | bytes 2359296 | tf_op jit(solution)/shard_map/psum | solution.py:387
  326.0 14.5 %collective-permute-start.16 = (bf16[768,768]{1,0:T(8,128)(2,1)}, bf16[768,768]{1,0:T(8,128)(2,1)}, u32[]{:S(2)}, u32[]{:S(2)}) collective-permute-start(bf16[768,768]{1,0:T(8,128)(2,1)} %get-tuple-element.156), channel_id=1, source_target_pairs={{0,16},{16,0},{1,17},{17,1},{2,18},{18,2},{3,19},{19,3},{4,20},{20... | collective-permute-start | bytes 3538952 | tf_op jit(solution)/shard_map/ppermute | solution.py:164
  335.3 3.5 collective-permute-start.14
  343.4 153.5 %all-reduce.10.cloned.1.call-start = ((), (), s32[]{:S(2)}) async-start(), calls=%async_computation.7 | async-start | bytes 2359296 | tf_op jit(solution)/shard_map/psum | solution.py:430
  416.5 18.1 %collective-permute-start.15 = (bf16[768,768]{1,0:T(8,128)(2,1)S(1)}, bf16[768,768]{1,0:T(8,128)(2,1)S(1)}, u32[]{:S(2)}, u32[]{:S(2)}) collective-permute-start(bf16[768,768]{1,0:T(8,128)(2,1)S(1)} %get-tuple-element.154), channel_id=1, source_target_pairs={{0,16},{16,0},{1,17},{17,1},{2,18},{18,2},{3,19},{19,3},{4,20},{20... | collective-permute-start | bytes 3538952 | tf_op jit(solution)/shard_map/ppermute | solution.py:164
  418.5 15.3 %collective-permute-start.13 = (bf16[384,576]{0,1:T(8,128)(2,1)S(1)}, bf16[384,576]{0,1:T(8,128)(2,1)S(1)}, u32[]{:S(2)}, u32[]{:S(2)}) collective-permute-start(bf16[384,576]{0,1:T(8,128)(2,1)S(1)} %broadcast_select_fusion.26), channel_id=1, source_target_pairs={{0,16},{16,0},{1,17},{17,1},{2,18},{18,2},{3,19},{19,3},{4,20},{20... | collective-permute-start | bytes 1327112 | tf_op jit(solution)/shard_map/ppermute | solution.py:164
  436.8 101.5 %reduce-scatter.5.cloned.1.call-start = ((), (), s32[]{:S(2)}) async-start(), calls=%async_computation.5 | async-start | bytes 2457600 | tf_op jit(solution)/shard_map/reduce_scatter | solution.py:187
  475.9 155.9 %all-reduce.12.cloned.1.call-start = ((), (), s32[]{:S(2)}) async-start(), calls=%async_computation.8 | async-start | bytes 2359296 | tf_op jit(solution)/shard_map/psum | solution.py:430
  489.5 9.9 %collective-permute-start.8 = (bf16[160,768]{1,0:T(8,128)(2,1)S(1)}, bf16[160,768]{1,0:T(8,128)(2,1)S(1)}, u32[]{:S(2)}, u32[]{:S(2)}) collective-permute-start(bf16[160,768]{1,0:T(8,128)(2,1)S(1)} %get-tuple-element.83), channel_id=1, source_target_pairs={{0,16},{16,0},{1,17},{17,1},{2,18},{18,2},{3,19},{19,3},{4,20},{20... | collective-permute-start | bytes 737288 | tf_op jit(solution)/shard_map/ppermute | solution.py:164
  499.3 5.2 collective-permute-start.19
  541.5 31.3 %collective-permute-start.11 = (bf16[384,576]{0,1:T(8,128)(2,1)}, bf16[384,576]{0,1:T(8,128)(2,1)}, u32[]{:S(2)}, u32[]{:S(2)}) collective-permute-start(bf16[384,576]{0,1:T(8,128)(2,1)} %broadcast_select_fusion.27), channel_id=1, source_target_pairs={{0,16},{16,0},{1,17},{17,1},{2,18},{18,2},{3,19},{19,3},{4,20},{20... | collective-permute-start | bytes 1327112 | tf_op jit(solution)/shard_map/ppermute | solution.py:164
  571.8 2.9 collective-permute-start.10
  572.2 4.9 collective-permute-start.9
  (121 other events, 1211.1 us)
Sparse Core Ops, SparseCore 0:
  30.3 45.2 all-gather.2
  149.3 61.7 all-gather.4
  320.7 58.0 reduce-scatter.2
  381.6 55.1 all-reduce.7
  439.6 55.4 all-reduce.9
  497.3 40.9 reduce-scatter.4
  574.8 56.9 all-reduce.11
